TPU v7x, 32 devices: a whole 2x2x4 slice. The times are simulated.
32 devices in a mesh: seq: 16 (over z, x, core), head: 2 (over y).
Axes of the slice: x: 2, y: 2, z: 4, core: 2. Of those that a mesh axis runs over, the one named last changes fastest.
Arguments:
- queries: bfloat16 [8192, 4096], P(('seq', 'head')), may hold values from -5 to 5
- new_keys: bfloat16 [8192, 1024], P(('seq', 'head')), may hold values from -12 to 12
- new_values: bfloat16 [8192, 1024], P(('seq', 'head')), may hold values from -6 to 6
- cache_keys: bfloat16 [32768, 1024], P('seq', 'head'), may hold values from -12 to 12
- cache_values: bfloat16 [32768, 1024], P('seq', 'head'), may hold values from -6 to 6
- tile_lists: int32 [64, 8, 12], P('seq', 'head'), may hold values from 0 to 255, as said below
Outputs:
- attended: bfloat16 [8192, 4096], P(('seq', 'head'))
Inputs may be any that keep to these rules, and one draw needn't show every extreme that they name: `tile_lists`: for one key head, the 12 tiles of one block's list are distinct; the lists of the 4 blocks of one index of seq together name exactly 24 distinct tiles, at most 2 of them of one index of seq (tiles k * 16 to k * 16 + 15), and some index has exactly 2.
All inputs are finite; a program needn't handle non-finite values.
Results may differ from a plain program's by a relative error of at most 0.003.
Values may be sent and summed in bfloat16 or wider, within the bound.
No kernel may reach another device: no remote copies, remote signals or barrier semaphores. Data moves between devices by JAX's collectives and lax.ppermute only.
A program may use at most 192 MiB of HBM per device.

v0:
```python
import math

import jax
import jax.numpy as jnp
from jax import lax
from jax.sharding import PartitionSpec as P

HQ = 32
KV = 8
HD = 128
QB = 128
TILE = 128
SEL = 12


NEG_FILL = -1e30


def passed_along(block, axis, distance):
    devices = range(lax.axis_size(axis))
    route = [(i - distance, i) for i in devices if i - distance in devices]
    return lax.ppermute(block, axis, route)


def pair_ranks(owners, tiles):
    pair_count = owners.shape[-1]
    earlier = jnp.arange(pair_count)[:, None] > jnp.arange(pair_count)[None, :]
    same_tile = tiles[..., :, None] == tiles[..., None, :]
    first_seen = jnp.logical_not(jnp.any(same_tile & earlier, axis=-1))
    same_owner = owners[..., :, None] == owners[..., None, :]
    smaller = tiles[..., None, :] < tiles[..., :, None]
    counted = same_owner & smaller & first_seen[..., None, :]
    return (jnp.sum(counted.astype(jnp.int32), axis=-1), first_seen)


def on_device(queries, new_keys, new_values, cache_keys, cache_values, tile_lists):
    q_rows, k_rows, v_rows = (
        lax.all_to_all(queries, "head", split_axis=1, concat_axis=0, tiled=True),
        lax.all_to_all(new_keys, "head", split_axis=1, concat_axis=0, tiled=True),
        lax.all_to_all(new_values, "head", split_axis=1, concat_axis=0, tiled=True),
    )
    rows_here = q_rows.shape[0]
    kv_here = k_rows.shape[1] // HD
    group_size = HQ // KV
    blocks_here = rows_here // QB
    tiles_here = cache_keys.shape[0] // TILE
    shards = lax.axis_size("seq")
    shard_index = lax.axis_index("seq")
    pair_total = blocks_here * SEL
    pool_size = max(SEL, pair_total // 2)
    capacity = max(2, (4 * pool_size + 3 * shards - 1) // (3 * shards))
    scale_factor = 1.0 / math.sqrt(HD)
    prior_keys, prior_values = passed_along(
        (k_rows[rows_here - QB :], v_rows[rows_here - QB :]), "seq", 1
    )
    pair_tiles = jnp.transpose(tile_lists, (1, 0, 2)).reshape(kv_here, pair_total)
    owners = pair_tiles // tiles_here
    pair_rank, first_seen = pair_ranks(owners, pair_tiles)
    every_list = lax.all_gather(tile_lists, "seq", axis=0, tiled=True)
    every_pair = jnp.transpose(
        every_list.reshape(shards, blocks_here, kv_here, SEL), (0, 2, 1, 3)
    ).reshape(shards, kv_here, pair_total)
    every_owner = every_pair // tiles_here
    every_rank, every_first = pair_ranks(every_owner, every_pair)
    own_hit = ((every_owner == shard_index) & every_first)[..., None]
    rank_hit = every_rank[..., None] == jnp.arange(capacity)
    marked = jnp.where(own_hit & rank_hit, (every_pair % tiles_here)[..., None] + 1, 0)
    asked_ids = jnp.sum(marked, axis=2) - 1
    head_pick = jnp.arange(kv_here)[None, :, None]
    filled = (asked_ids >= 0)[..., None, None]
    safe_ids = jnp.maximum(asked_ids, 0)
    key_tiles = jnp.transpose(cache_keys.reshape(tiles_here, TILE, kv_here, HD), (2, 0, 1, 3))
    value_tiles = jnp.transpose(cache_values.reshape(tiles_here, TILE, kv_here, HD), (2, 0, 1, 3))
    send_keys = jnp.where(filled, key_tiles[head_pick, safe_ids], jnp.zeros((), jnp.bfloat16))
    send_values = jnp.where(filled, value_tiles[head_pick, safe_ids], jnp.zeros((), jnp.bfloat16))
    causal = jnp.arange(QB)[:, None] >= jnp.arange(QB)[None, :]
    head_rows = jnp.arange(kv_here)[:, None]

    def local_part(block_index, source, prior_rows):
        current = lax.dynamic_slice_in_dim(source, block_index * QB, QB, 0)
        before_rows = lax.dynamic_slice_in_dim(source, jnp.maximum(block_index - 1, 0) * QB, QB, 0)
        previous = jnp.where(block_index == 0, prior_rows, before_rows)
        joined = jnp.concatenate([previous, current], axis=0).reshape(2 * QB, kv_here, HD)
        return jnp.transpose(joined, (1, 0, 2))

    def remote_part(block_index, received):
        block_owners = lax.dynamic_slice_in_dim(owners, block_index * SEL, SEL, 1)
        block_ranks = lax.dynamic_slice_in_dim(pair_rank, block_index * SEL, SEL, 1)
        return received[block_owners, head_rows, block_ranks].reshape(kv_here, SEL * TILE, HD)

    def block_weights(block_index, got_keys):
        query_block = lax.dynamic_slice_in_dim(q_rows, block_index * QB, QB, 0).reshape(
            QB, kv_here, group_size, HD
        )
        all_keys = jnp.concatenate(
            [remote_part(block_index, got_keys), local_part(block_index, k_rows, prior_keys)],
            axis=1,
        )
        scores = (
            jnp.einsum("qhgd,hkd->hgqk", query_block, all_keys, preferred_element_type=jnp.float32)
            * scale_factor
        )
        has_prior = jnp.broadcast_to((block_index > 0) | (shard_index > 0), (QB, QB))
        visible = jnp.concatenate(
            [jnp.ones((QB, SEL * TILE), dtype=bool), has_prior, causal], axis=1
        )
        masked = jnp.where(visible, scores, NEG_FILL)
        row_top = jnp.max(masked, axis=3, keepdims=True)
        exponent = jnp.exp(masked - row_top)
        row_total = jnp.sum(exponent, axis=3)
        return (exponent.astype(jnp.bfloat16), row_total)

    def block_output(block_index, weights, row_total, got_values):
        all_values = jnp.concatenate(
            [remote_part(block_index, got_values), local_part(block_index, v_rows, prior_values)],
            axis=1,
        )
        weighted = jnp.einsum(
            "hgqk,hkd->qhgd", weights, all_values, preferred_element_type=jnp.float32
        )
        result = weighted / jnp.transpose(row_total, (2, 0, 1))[..., None]
        return result.astype(jnp.bfloat16).reshape(QB, kv_here * group_size * HD)

    block_ids = jnp.arange(blocks_here)
    got_keys = lax.all_to_all(send_keys, "seq", split_axis=0, concat_axis=0, tiled=True)
    all_weights, all_totals = lax.map(
        lambda block_index: block_weights(block_index, got_keys), block_ids
    )
    got_values = lax.all_to_all(send_values, "seq", split_axis=0, concat_axis=0, tiled=True)

    def finish_block(packed):
        return block_output(packed[0], packed[1], packed[2], got_values)

    outputs = lax.map(finish_block, (block_ids, all_weights, all_totals))
    attended = outputs.reshape(rows_here, kv_here * group_size * HD)
    return lax.all_to_all(attended, "head", split_axis=0, concat_axis=1, tiled=True)


def solution(mesh):
    return jax.shard_map(
        on_device,
        mesh=mesh,
        in_specs=(
            P(("seq", "head"), None),
            P(("seq", "head"), None),
            P(("seq", "head"), None),
            P("seq", "head"),
            P("seq", "head"),
            P("seq", "head", None),
        ),
        out_specs=P(("seq", "head"), None),
        check_vma=False,
    )
```

profile of v0, /device:TPU:0, one launch (start us, length us, event | category | flops | bytes accessed | tf_op | source)
XLA Modules:
  0.0 453.2 jit_solution(11545753127082541569)
XLA Ops:
  0.0 2.2 copy.173
  2.2 4.2 all-to-all-start.3
  6.4 22.9 %all_gather.3 = s32[64,4,12]{2,1,0:T(4,128)S(1)} all-gather(s32[4,4,12]{2,1,0:T(4,128)} %param.15), channel_id=1, replica_groups=mesh['seq'=16,'head'=2] {'seq'}, dimensions={0}, use_global_device_ids=true | all-gather | bytes 13056 | tf_op jit(solution)/shard_map/all_gather | solution.py:59
  29.6 1.7 and_reduce_fusion
  31.4 2.4 convert_reduce_fusion
  33.8 2.5 copy.175
  36.3 1.0 copy.169
  37.3 3.5 all-to-all-start.1
  41.0 8.8 %all-to-all-done.1 = bf16[256,2,512]{0,2,1:T(8,128)(2,1)S(1)} async-done(((bf16[256,2,512]{0,2,1:T(8,128)(2,1)}), bf16[256,2,512]{0,2,1:T(8,128)(2,1)S(1)}, u32[]{:S(2)}, u32[]{:S(2)}) %all-to-all-start.1) | async-done | bytes 524320 | tf_op jit(solution)/shard_map/all_to_all | solution.py:40
  49.8 4.8 %all-to-all-start.4 = ((bf16[256,2,2048]{0,2,1:T(8,128)(2,1)}), bf16[256,2,2048]{0,2,1:T(8,128)(2,1)}, u32[]{:S(2)}, u32[]{:S(2)}) async-start(bf16[256,2,2048]{0,2,1:T(8,128)(2,1)} %bitcast.16), calls=%async_computation.4 | async-start | bytes 4194304 | tf_op jit(solution)/shard_map/all_to_all | solution.py:38
  54.9 2.0 reshape.411
  56.9 2.1 copy.209
  59.1 4.0 reshape.412
  63.0 3.4 copy.208
  66.5 3.1 gather_fusion.2
  69.6 4.6 %gather_fusion.3 = bf16[128,128,128]{2,1,0:T(8,128)(2,1)} fusion(bf16[4,16,128,128]{3,2,1,0:T(8,128)(2,1)} %bitcast.186, s32[128]{0:T(128)S(1)} %reshape.353), kind=kCustom, calls=%fused_computation.3 | custom fusion | bytes 8389632 | tf_op jit(solution)/shard_map/gather | solution.py:74
  74.4 5.8 %broadcast_select_fusion = (bf16[16,4,2,128,128]{4,3,2,1,0:T(8,128)(2,1)}, bf16[16,4,2,128,128]{4,3,2,1,0:T(8,128)(2,1)}) fusion(bf16[16,4,2,128,128]{4,3,2,1,0:T(8,128)(2,1)} %bitcast.188, pred[16,4,2]{2,1,0:T(4,128)(4,1)S(1)} %copy.165, bf16[16,4,2,128,128]{4,3,2,1,0:T(8,128)(2,1)} %bitcast.187), kind=kLoop, calls=%fused_computation.69 | loop fusion | flops 4194304 | bytes 16777344 | tf_op jit(solution)/shard_map/jit(_where)/select_n | solution.py:74
  80.1 4.6 %all-to-all-start.2 = ((bf16[16,4,2,128,128]{4,3,2,1,0:T(8,128)(2,1)}), bf16[16,4,2,128,128]{4,3,2,1,0:T(8,128)(2,1)}, u32[]{:S(2)}, u32[]{:S(2)}) async-start(bf16[16,4,2,128,128]{4,3,2,1,0:T(8,128)(2,1)} %get-tuple-element.509), calls=%async_computation.2 | async-start | bytes 8388608 | tf_op jit(solution)/shard_map/all_to_all | solution.py:125
  85.1 2.1 collective-permute-start.1
  87.4 3.5 collective-permute-start
  91.7 1.0 copy.180
  93.0 2.9 copy.176
  96.0 66.3 %all-to-all-done.2 = bf16[16,4,2,128,128]{4,3,2,1,0:T(8,128)(2,1)} async-done(((bf16[16,4,2,128,128]{4,3,2,1,0:T(8,128)(2,1)}), bf16[16,4,2,128,128]{4,3,2,1,0:T(8,128)(2,1)}, u32[]{:S(2)}, u32[]{:S(2)}) %all-to-all-start.2) | async-done | bytes 4194336 | tf_op jit(solution)/shard_map/all_to_all | solution.py:125
  162.3 25.0 %all-to-all-start = ((bf16[16,4,2,128,128]{4,3,2,1,0:T(8,128)(2,1)}), bf16[16,4,2,128,128]{4,3,2,1,0:T(8,128)(2,1)}, u32[]{:S(2)}, u32[]{:S(2)}) async-start(bf16[16,4,2,128,128]{4,3,2,1,0:T(8,128)(2,1)} %get-tuple-element.510), calls=%async_computation | async-start | bytes 8388608 | tf_op jit(solution)/shard_map/all_to_all | solution.py:129
  187.3 171.3 %while.28 = (s32[]{:T(128)}, bf16[4,4,4,128,1792]{3,4,2,1,0:T(8,128)(2,1)}, f32[4,4,4,128]{3,2,1,0:T(4,128)}, s32[4]{0:T(128)S(1)}, pred[]{:T(512)}, /*index=5*/...) while((s32[]{:T(128)}, ...), condition=%wide.region_8.9_spmd.clone, body=%wide.region_5.8_spmd.clone.sunk | while | flops 969723968 | bytes 112822120 | solution.py:126
  191.4 3.3 gather_fusion
  194.8 7.3 %fusion.65 = f32[4,1792,128,4]{2,1,3,0:T(8,128)} fusion(bf16[128,4,4,128]{0,3,2,1:T(8,128)(2,1)S(1)} %bitcast.182, bf16[4,256,128]{2,1,0:T(8,128)(2,1)S(1)} %bitcast.183, bf16[4,1536,128]{2,1,0:T(8,128)(2,1)S(1)} %bitcast.180), kind=kOutput, calls=%fused_computation.16.clone.1 | convolution fusion | flops 943194112 | bytes 17039360 | tf_op jit(solution)/shard_map/while/body/eval_jaxpr/qhgd,hkd->hgqk/dot_general | solution.py:100
  203.0 20.5 %bitcast_dynamic-update-slice_fusion.4 = (bf16[4,4,4,128,1792]{3,4,2,1,0:T(8,128)(2,1)}, f32[4,4,128,1792]{2,3,1,0:T(8,128)}) fusion(bf16[4,4,4,128,1792]{3,4,2,1,0:T(8,128)(2,1)} %get-tuple-element.674, s32[]{:T(128)} %get-tuple-element.673, f32[4,1792,128,4]{2,1,3,0:T(8,128)} %fusion.65, pred[128,1792]{0,1:T(8,128)(4,1)S(1)} %pad_add_fusion.5), kind=kOutput, calls=%fused_computation.11.clone.1 | output fusion | flops 22023936 | bytes 51839488 | tf_op jit(solution)/shard_map/while/body/eval_jaxpr/sub | solution.py:109
  223.5 6.0 %reduce_sum.47 = f32[4,4,128]{2,1,0:T(4,128)S(1)} reduce(f32[4,4,128,1792]{2,3,1,0:T(8,128)} %get-tuple-element.639, f32[]{:T(128)} %constant.197.clone.2..sunk), dimensions={3}, to_apply=%region_7.7 | reduce | flops 3667968 | bytes 14688260 | tf_op jit(solution)/shard_map/while/body/eval_jaxpr/reduce_sum | solution.py:110
  234.2 3.3 gather_fusion
  237.5 7.3 %fusion.65 = f32[4,1792,128,4]{2,1,3,0:T(8,128)} fusion(bf16[128,4,4,128]{0,3,2,1:T(8,128)(2,1)S(1)} %bitcast.182, bf16[4,256,128]{2,1,0:T(8,128)(2,1)S(1)} %bitcast.183, bf16[4,1536,128]{2,1,0:T(8,128)(2,1)S(1)} %bitcast.180), kind=kOutput, calls=%fused_computation.16.clone.1 | convolution fusion | flops 943194112 | bytes 17039360 | tf_op jit(solution)/shard_map/while/body/eval_jaxpr/qhgd,hkd->hgqk/dot_general | solution.py:100
  245.8 20.7 %bitcast_dynamic-update-slice_fusion.4 = (bf16[4,4,4,128,1792]{3,4,2,1,0:T(8,128)(2,1)}, f32[4,4,128,1792]{2,3,1,0:T(8,128)}) fusion(bf16[4,4,4,128,1792]{3,4,2,1,0:T(8,128)(2,1)} %get-tuple-element.674, s32[]{:T(128)} %get-tuple-element.673, f32[4,1792,128,4]{2,1,3,0:T(8,128)} %fusion.65, pred[128,1792]{0,1:T(8,128)(4,1)S(1)} %pad_add_fusion.5), kind=kOutput, calls=%fused_computation.11.clone.1 | output fusion | flops 22023936 | bytes 51839488 | tf_op jit(solution)/shard_map/while/body/eval_jaxpr/sub | solution.py:109
  266.5 6.0 %reduce_sum.47 = f32[4,4,128]{2,1,0:T(4,128)S(1)} reduce(f32[4,4,128,1792]{2,3,1,0:T(8,128)} %get-tuple-element.639, f32[]{:T(128)} %constant.197.clone.2..sunk), dimensions={3}, to_apply=%region_7.7 | reduce | flops 3667968 | bytes 14688260 | tf_op jit(solution)/shard_map/while/body/eval_jaxpr/reduce_sum | solution.py:110
  277.1 3.3 gather_fusion
  280.5 7.3 %fusion.65 = f32[4,1792,128,4]{2,1,3,0:T(8,128)} fusion(bf16[128,4,4,128]{0,3,2,1:T(8,128)(2,1)S(1)} %bitcast.182, bf16[4,256,128]{2,1,0:T(8,128)(2,1)S(1)} %bitcast.183, bf16[4,1536,128]{2,1,0:T(8,128)(2,1)S(1)} %bitcast.180), kind=kOutput, calls=%fused_computation.16.clone.1 | convolution fusion | flops 943194112 | bytes 17039360 | tf_op jit(solution)/shard_map/while/body/eval_jaxpr/qhgd,hkd->hgqk/dot_general | solution.py:100
  288.8 20.5 %bitcast_dynamic-update-slice_fusion.4 = (bf16[4,4,4,128,1792]{3,4,2,1,0:T(8,128)(2,1)}, f32[4,4,128,1792]{2,3,1,0:T(8,128)}) fusion(bf16[4,4,4,128,1792]{3,4,2,1,0:T(8,128)(2,1)} %get-tuple-element.674, s32[]{:T(128)} %get-tuple-element.673, f32[4,1792,128,4]{2,1,3,0:T(8,128)} %fusion.65, pred[128,1792]{0,1:T(8,128)(4,1)S(1)} %pad_add_fusion.5), kind=kOutput, calls=%fused_computation.11.clone.1 | output fusion | flops 22023936 | bytes 51839488 | tf_op jit(solution)/shard_map/while/body/eval_jaxpr/sub | solution.py:109
  309.3 6.0 %reduce_sum.47 = f32[4,4,128]{2,1,0:T(4,128)S(1)} reduce(f32[4,4,128,1792]{2,3,1,0:T(8,128)} %get-tuple-element.639, f32[]{:T(128)} %constant.197.clone.2..sunk), dimensions={3}, to_apply=%region_7.7 | reduce | flops 3667968 | bytes 14688260 | tf_op jit(solution)/shard_map/while/body/eval_jaxpr/reduce_sum | solution.py:110
  319.9 3.3 gather_fusion
  323.3 7.3 %fusion.65 = f32[4,1792,128,4]{2,1,3,0:T(8,128)} fusion(bf16[128,4,4,128]{0,3,2,1:T(8,128)(2,1)S(1)} %bitcast.182, bf16[4,256,128]{2,1,0:T(8,128)(2,1)S(1)} %bitcast.183, bf16[4,1536,128]{2,1,0:T(8,128)(2,1)S(1)} %bitcast.180), kind=kOutput, calls=%fused_computation.16.clone.1 | convolution fusion | flops 943194112 | bytes 17039360 | tf_op jit(solution)/shard_map/while/body/eval_jaxpr/qhgd,hkd->hgqk/dot_general | solution.py:100
  331.5 20.5 %bitcast_dynamic-update-slice_fusion.4 = (bf16[4,4,4,128,1792]{3,4,2,1,0:T(8,128)(2,1)}, f32[4,4,128,1792]{2,3,1,0:T(8,128)}) fusion(bf16[4,4,4,128,1792]{3,4,2,1,0:T(8,128)(2,1)} %get-tuple-element.674, s32[]{:T(128)} %get-tuple-element.673, f32[4,1792,128,4]{2,1,3,0:T(8,128)} %fusion.65, pred[128,1792]{0,1:T(8,128)(4,1)S(1)} %pad_add_fusion.5), kind=kOutput, calls=%fused_computation.11.clone.1 | output fusion | flops 22023936 | bytes 51839488 | tf_op jit(solution)/shard_map/while/body/eval_jaxpr/sub | solution.py:109
  352.1 6.0 %reduce_sum.47 = f32[4,4,128]{2,1,0:T(4,128)S(1)} reduce(f32[4,4,128,1792]{2,3,1,0:T(8,128)} %get-tuple-element.639, f32[]{:T(128)} %constant.197.clone.2..sunk), dimensions={3}, to_apply=%region_7.7 | reduce | flops 3667968 | bytes 14688260 | tf_op jit(solution)/shard_map/while/body/eval_jaxpr/reduce_sum | solution.py:110
  358.7 58.3 %while.29 = (s32[]{:T(128)}, bf16[4,128,2048]{2,1,0:T(8,128)(2,1)}, s32[4]{0:T(128)S(1)}, s32[4,48]{1,0:T(4,128)S(1)}, s32[4,48]{1,0:T(4,128)S(1)}, /*index=5*/b...) while((s32[]{:T(128)}, bf16[4,128,2048]{2,1,0:T(8,128)(2,1)}, ...), condition=%wide.region_10.11_spmd.clone, body=%wide.region_9.10_spmd.clone.sunk | while | flops 944308800 | bytes 19295116 | solution.py:134
  361.2 1.0 dynamic-slice_select_fusion.5
  363.0 3.3 gather_fusion.1
  367.1 0.7 dynamic-slice_bitcast_fusion.2
  367.8 4.4 divide_convert_fusion.2
  372.4 0.8 constant_dynamic-update-slice_fusion.2
  375.8 1.0 dynamic-slice_select_fusion.5
  377.6 3.3 gather_fusion.1
  382.4 4.4 divide_convert_fusion.2
  387.0 0.8 constant_dynamic-update-slice_fusion.2
  390.3 1.0 dynamic-slice_select_fusion.5
  392.2 3.3 gather_fusion.1
  396.2 0.7 dynamic-slice_bitcast_fusion.2
  396.9 4.4 divide_convert_fusion.2
  401.6 0.8 constant_dynamic-update-slice_fusion.2
  404.9 1.0 dynamic-slice_select_fusion.5
  406.8 3.3 gather_fusion.1
  410.8 0.7 dynamic-slice_bitcast_fusion.2
  411.5 4.4 divide_convert_fusion.2
  416.2 0.8 constant_dynamic-update-slice_fusion.2
  417.0 29.6 %all_to_all.86 = bf16[2,256,2048]{2,1,0:T(8,128)(2,1)S(1)} all-to-all(bf16[2,256,2048]{2,1,0:T(8,128)(2,1)} %bitcast.198), channel_id=1, replica_groups=mesh['seq'=16,'head'=2] {'head'}, dimensions={0} | all-to-all | bytes 4194304 | tf_op jit(solution)/shard_map/all_to_all | solution.py:136
  446.6 2.5 copy.184
  449.1 4.1 copy.185
  (183 shorter events, 19.5 us)
Async XLA Ops:
  0.0 33.8 %copy-start.6 = (bf16[256,4096]{1,0:T(8,128)(2,1)S(1)}, bf16[256,4096]{1,0:T(8,128)(2,1)}, u32[]{:S(2)}) copy-start(bf16[256,4096]{1,0:T(8,128)(2,1)} %param.10) | copy-start | bytes 6291460
  0.0 36.3 %copy-start.8 = (bf16[256,1024]{1,0:T(8,128)(2,1)S(1)}, bf16[256,1024]{1,0:T(8,128)(2,1)}, u32[]{:S(2)}) copy-start(bf16[256,1024]{1,0:T(8,128)(2,1)} %param.12) | copy-start | bytes 1572868
  2.2 35.1 %all-to-all-start.3 = ((bf16[256,2,512]{0,2,1:T(8,128)(2,1)}), bf16[256,2,512]{0,2,1:T(8,128)(2,1)S(1)}, u32[]{:S(2)}, u32[]{:S(2)}) async-start(bf16[256,2,512]{0,2,1:T(8,128)(2,1)} %bitcast.12), calls=%async_computation.3 | async-start | bytes 1048576 | tf_op jit(solution)/shard_map/all_to_all | solution.py:39
  36.3 18.6 %copy-start.7 = (bf16[2048,512]{1,0:T(8,128)(2,1)S(1)}, bf16[2048,512]{1,0:T(8,128)(2,1)}, u32[]{:S(2)}) copy-start(bf16[2048,512]{1,0:T(8,128)(2,1)} %param.14) | copy-start | bytes 6291460
  37.3 12.5 %all-to-all-start.1 = ((bf16[256,2,512]{0,2,1:T(8,128)(2,1)}), bf16[256,2,512]{0,2,1:T(8,128)(2,1)S(1)}, u32[]{:S(2)}, u32[]{:S(2)}) async-start(bf16[256,2,512]{0,2,1:T(8,128)(2,1)} %bitcast.199), calls=%async_computation.1 | async-start | bytes 1048576 | tf_op jit(solution)/shard_map/all_to_all | solution.py:40
  49.8 30.3 %all-to-all-start.4 = ((bf16[256,2,2048]{0,2,1:T(8,128)(2,1)}), bf16[256,2,2048]{0,2,1:T(8,128)(2,1)}, u32[]{:S(2)}, u32[]{:S(2)}) async-start(bf16[256,2,2048]{0,2,1:T(8,128)(2,1)} %bitcast.16), calls=%async_computation.4 | async-start | bytes 4194304 | tf_op jit(solution)/shard_map/all_to_all | solution.py:38
  80.1 4.6 %copy-start.9 = (s32[4,4,12]{2,1,0:T(4,128)S(1)}, s32[4,4,12]{2,1,0:T(4,128)}, u32[]{:S(2)}) copy-start(s32[4,4,12]{2,1,0:T(4,128)} %param.15) | copy-start | bytes 2308
  80.1 82.2 %all-to-all-start.2 = ((bf16[16,4,2,128,128]{4,3,2,1,0:T(8,128)(2,1)}), bf16[16,4,2,128,128]{4,3,2,1,0:T(8,128)(2,1)}, u32[]{:S(2)}, u32[]{:S(2)}) async-start(bf16[16,4,2,128,128]{4,3,2,1,0:T(8,128)(2,1)} %get-tuple-element.509), calls=%async_computation.2 | async-start | bytes 8388608 | tf_op jit(solution)/shard_map/all_to_all | solution.py:125
  85.1 7.7 %collective-permute-start.1 = (bf16[128,512]{1,0:T(8,128)(2,1)S(1)}, bf16[128,512]{1,0:T(8,128)(2,1)S(1)}, u32[]{:S(2)}, u32[]{:S(2)}) collective-permute-start(bf16[128,512]{1,0:T(8,128)(2,1)S(1)} %slice.19), channel_id=1, source_target_pairs={{0,2},{2,4},{4,6},{6,8},{8,10},{10,12},{12,14},{14,16},{16,18},{18... | collective-permute-start | bytes 393224 | tf_op jit(solution)/shard_map/ppermute | solution.py:22
  87.4 5.4 %collective-permute-start = (bf16[128,512]{1,0:T(8,128)(2,1)S(1)}, bf16[128,512]{1,0:T(8,128)(2,1)S(1)}, u32[]{:S(2)}, u32[]{:S(2)}) collective-permute-start(bf16[128,512]{1,0:T(8,128)(2,1)S(1)} %slice.18), channel_id=1, source_target_pairs={{0,2},{2,4},{4,6},{6,8},{8,10},{10,12},{12,14},{14,16},{16,18},{18... | collective-permute-start | bytes 393224 | tf_op jit(solution)/shard_map/ppermute | solution.py:22
  162.3 196.4 %all-to-all-start = ((bf16[16,4,2,128,128]{4,3,2,1,0:T(8,128)(2,1)}), bf16[16,4,2,128,128]{4,3,2,1,0:T(8,128)(2,1)}, u32[]{:S(2)}, u32[]{:S(2)}) async-start(bf16[16,4,2,128,128]{4,3,2,1,0:T(8,128)(2,1)} %get-tuple-element.510), calls=%async_computation | async-start | bytes 8388608 | tf_op jit(solution)/shard_map/all_to_all | solution.py:129
  187.4 2.7 copy-start.2
  187.4 2.9 copy-start.4
  187.4 3.9 copy-start
  223.5 6.6 %copy-start.1 = (bf16[512,2048]{1,0:T(8,128)(2,1)S(1)}, bf16[512,2048]{1,0:T(8,128)(2,1)}, u32[]{:S(2)}) copy-start(bf16[512,2048]{1,0:T(8,128)(2,1)} %copy-done) | copy-start | bytes 6291460 | tf_op jit(solution)/shard_map/while
  223.5 6.6 %copy-start.3 = (bf16[512,512]{0,1:T(8,128)(2,1)S(1)}, bf16[512,512]{0,1:T(8,128)(2,1)}, u32[]{:S(2)}) copy-start(bf16[512,512]{0,1:T(8,128)(2,1)} %copy-done.2) | copy-start | bytes 1572868 | tf_op jit(solution)/shard_map/while
  223.5 6.6 %copy-start.5 = (bf16[128,512]{0,1:T(8,128)(2,1)S(1)}, bf16[128,512]{0,1:T(8,128)(2,1)}, u32[]{:S(2)}) copy-start(bf16[128,512]{0,1:T(8,128)(2,1)} %copy-done.4) | copy-start | bytes 393220 | tf_op jit(solution)/shard_map/while
  230.1 2.7 copy-start.2
  230.1 2.9 copy-start.4
  230.1 3.9 copy-start
  266.5 6.6 %copy-start.1 = (bf16[512,2048]{1,0:T(8,128)(2,1)S(1)}, bf16[512,2048]{1,0:T(8,128)(2,1)}, u32[]{:S(2)}) copy-start(bf16[512,2048]{1,0:T(8,128)(2,1)} %copy-done) | copy-start | bytes 6291460 | tf_op jit(solution)/shard_map/while
  266.5 6.6 %copy-start.3 = (bf16[512,512]{0,1:T(8,128)(2,1)S(1)}, bf16[512,512]{0,1:T(8,128)(2,1)}, u32[]{:S(2)}) copy-start(bf16[512,512]{0,1:T(8,128)(2,1)} %copy-done.2) | copy-start | bytes 1572868 | tf_op jit(solution)/shard_map/while
  266.5 6.6 %copy-start.5 = (bf16[128,512]{0,1:T(8,128)(2,1)S(1)}, bf16[128,512]{0,1:T(8,128)(2,1)}, u32[]{:S(2)}) copy-start(bf16[128,512]{0,1:T(8,128)(2,1)} %copy-done.4) | copy-start | bytes 393220 | tf_op jit(solution)/shard_map/while
  273.1 2.7 copy-start.2
  273.1 2.9 copy-start.4
  273.1 3.9 copy-start
  309.3 6.6 %copy-start.1 = (bf16[512,2048]{1,0:T(8,128)(2,1)S(1)}, bf16[512,2048]{1,0:T(8,128)(2,1)}, u32[]{:S(2)}) copy-start(bf16[512,2048]{1,0:T(8,128)(2,1)} %copy-done) | copy-start | bytes 6291460 | tf_op jit(solution)/shard_map/while
  309.3 6.6 %copy-start.3 = (bf16[512,512]{0,1:T(8,128)(2,1)S(1)}, bf16[512,512]{0,1:T(8,128)(2,1)}, u32[]{:S(2)}) copy-start(bf16[512,512]{0,1:T(8,128)(2,1)} %copy-done.2) | copy-start | bytes 1572868 | tf_op jit(solution)/shard_map/while
  309.3 6.6 %copy-start.5 = (bf16[128,512]{0,1:T(8,128)(2,1)S(1)}, bf16[128,512]{0,1:T(8,128)(2,1)}, u32[]{:S(2)}) copy-start(bf16[128,512]{0,1:T(8,128)(2,1)} %copy-done.4) | copy-start | bytes 393220 | tf_op jit(solution)/shard_map/while
  315.9 2.7 copy-start.2
  315.9 2.9 copy-start.4
  315.9 3.9 copy-start
  352.1 6.6 %copy-start.1 = (bf16[512,2048]{1,0:T(8,128)(2,1)S(1)}, bf16[512,2048]{1,0:T(8,128)(2,1)}, u32[]{:S(2)}) copy-start(bf16[512,2048]{1,0:T(8,128)(2,1)} %copy-done) | copy-start | bytes 6291460 | tf_op jit(solution)/shard_map/while
  352.1 6.6 %copy-start.3 = (bf16[512,512]{0,1:T(8,128)(2,1)S(1)}, bf16[512,512]{0,1:T(8,128)(2,1)}, u32[]{:S(2)}) copy-start(bf16[512,512]{0,1:T(8,128)(2,1)} %copy-done.2) | copy-start | bytes 1572868 | tf_op jit(solution)/shard_map/while
  352.1 6.6 %copy-start.5 = (bf16[128,512]{0,1:T(8,128)(2,1)S(1)}, bf16[128,512]{0,1:T(8,128)(2,1)}, u32[]{:S(2)}) copy-start(bf16[128,512]{0,1:T(8,128)(2,1)} %copy-done.4) | copy-start | bytes 393220 | tf_op jit(solution)/shard_map/while
where the time goes:
time: 455 us; the launch traced here: 453 us
  other arithmetic  123 us (27%)
  local copies, waits for them, and re-layouts  83.9 us (18%)
  waiting for transfers between devices  75.1 us (17%)
  blocking collectives  52.6 us (12%)
  starting transfers between devices  47.8 us (11%)
  matrix products  46.8 us (10%)
  loops' own time  23.4 us (5%)
    sub x4, other arithmetic, block_weights(): exponent = jnp.exp(masked - row_top)  82.2 us
    all_to_all x1, waiting for transfers between devices, on_device(): lax.all_to_all(send_keys, 'seq', split_axis=0, concat_axis=0, tiled=True)  66.3 us
    all_to_all x1, blocking collectives, on_device(): lax.all_to_all(attended, 'head', split_axis=0, concat_axis=1, tiled=True)  29.6 us
    dot_general x4, matrix products, block_weights(): jnp.einsum('qhgd,hkd->hgqk', query_block, all_keys, preferred_element_typ...  29.1 us
    gather x8, local copies, waits for them, and re-layouts, remote_part(): received[block_owners, head_rows, block_ranks]  26.7 us
    all_to_all x1, starting transfers between devices, on_device(): lax.all_to_all(send_values, 'seq', split_axis=0, concat_axis=0, tiled=True)  25 us
    reduce_sum x4, other arithmetic, block_weights(): row_total = jnp.sum(exponent, axis=3)  23.9 us
    all_gather x1, blocking collectives, on_device(): every_list = lax.all_gather(tile_lists, 'seq', axis=0, tiled=True)  22.9 us
  transfers between devices with their start and end apart: 7, of which 2 were waited for; matrix products, arithmetic and copies ran while one was open for 43% of the time, Pallas kernels for 0%

commit v1 on v0

v1 whole, which is shorter than its diff:
```python
import functools
import math

import jax
import jax.numpy as jnp
from jax import lax
from jax.experimental import pallas as pl
from jax.experimental.pallas import tpu as pltpu
from jax.sharding import PartitionSpec as P

HQ = 32
KV = 8
HD = 128
QB = 128
TILE = 128
SEL = 12
RANKS = 2
GROUP = HQ // KV
NEG_FILL = -1e30
VMEM_LIMIT = 50 * 1024 * 1024


def swap_heads(rows, n_head, me):
    if n_head != 2:
        return lax.all_to_all(rows, "head", split_axis=1, concat_axis=0, tiled=True)
    width = rows.shape[1] // 2
    kept = lax.dynamic_slice_in_dim(rows, me * width, width, 1)
    sent = lax.dynamic_slice_in_dim(rows, (1 - me) * width, width, 1)
    got = lax.ppermute(sent, "head", [(0, 1), (1, 0)])
    return jnp.where(
        me == 0, jnp.concatenate([kept, got], axis=0), jnp.concatenate([got, kept], axis=0)
    )


def swap_back(outs, n_head, me):
    width = sum(o.shape[1] for o in outs)
    rows = outs[0].shape[0] // n_head
    if n_head != 2:
        whole = jnp.concatenate(outs, axis=1)
        return lax.all_to_all(whole, "head", split_axis=0, concat_axis=1, tiled=True)
    result = jnp.zeros((rows, 2 * width), outs[0].dtype)
    at = 0
    for o in outs:
        kept = lax.dynamic_slice_in_dim(o, me * rows, rows, 0)
        sent = lax.dynamic_slice_in_dim(o, (1 - me) * rows, rows, 0)
        got = lax.ppermute(sent, "head", [(0, 1), (1, 0)])
        result = lax.dynamic_update_slice(result, kept, (0, me * width + at))
        result = lax.dynamic_update_slice(result, got, (0, (1 - me) * width + at))
        at += o.shape[1]
    return result


def gather_kernel(first, heads, asked, keys, values, out, sem):
    shards = out.shape[0]

    def one(i, carry):
        peer = i // (heads * RANKS)
        rest = i % (heads * RANKS)
        head = rest // RANKS
        rank = rest % RANKS
        tile = asked[peer, (first + head) * RANKS + rank]
        rows = pl.ds(pl.multiple_of(tile * TILE, TILE), TILE)
        cols = pl.ds(pl.multiple_of((first + head) * HD, HD), HD)
        pltpu.make_async_copy(keys.at[rows, cols], out.at[peer, head, rank, 0], sem).start()
        pltpu.make_async_copy(values.at[rows, cols], out.at[peer, head, rank, 1], sem).start()
        return carry

    lax.fori_loop(0, shards * heads * RANKS, one, 0)
    pltpu.make_async_copy(out, out, sem).wait()


def gather_tiles(asked, keys, values, first, heads):
    shards = asked.shape[0]
    shape = (shards, heads, RANKS, 2, TILE, HD)
    return pl.pallas_call(
        functools.partial(gather_kernel, first, heads),
        out_shape=jax.ShapeDtypeStruct(shape, jnp.bfloat16),
        grid_spec=pltpu.PrefetchScalarGridSpec(
            num_scalar_prefetch=1,
            grid=(),
            in_specs=[pl.BlockSpec(memory_space=pl.ANY)] * 2,
            out_specs=pl.BlockSpec(memory_space=pl.ANY),
            scratch_shapes=[pltpu.SemaphoreType.DMA],
        ),
        cost_estimate=pl.CostEstimate(
            flops=0, bytes_accessed=4 * math.prod(shape), transcendentals=0
        ),
        name="gather_tiles",
    )(asked, keys, values)


def attend_kernel(
    first, slots, info, q_ref, tiles, k_rows, v_rows, k_prior, v_prior, out, k_all, v_all
):
    head = pl.program_id(0)
    block = pl.program_id(1)
    blocks = pl.num_programs(1)
    listed = SEL * TILE
    for j in range(SEL):
        slot = slots[((first + head) * blocks + block) * SEL + j]
        owner = slot // RANKS
        rank = slot % RANKS
        k_all[j * TILE : (j + 1) * TILE, :] = tiles[owner, 0, rank, 0]
        v_all[j * TILE : (j + 1) * TILE, :] = tiles[owner, 0, rank, 1]
    here = pl.ds(pl.multiple_of(block * QB, QB), QB)
    before = pl.ds(pl.multiple_of(jnp.maximum(block - 1, 0) * QB, QB), QB)

    @pl.when(block == 0)
    def _():
        k_all[listed : listed + QB, :] = k_prior[...]
        v_all[listed : listed + QB, :] = v_prior[...]

    @pl.when(block > 0)
    def _():
        k_all[listed : listed + QB, :] = k_rows[before, :]
        v_all[listed : listed + QB, :] = v_rows[before, :]

    k_all[listed + QB :, :] = k_rows[here, :]
    v_all[listed + QB :, :] = v_rows[here, :]
    has_prior = (block > 0) | (info[0] > 0)
    scale = 1.0 / math.sqrt(HD)
    causal = lax.broadcasted_iota(jnp.int32, (QB, QB), 0) >= lax.broadcasted_iota(
        jnp.int32, (QB, QB), 1
    )
    for g in range(GROUP):
        q = q_ref[:, g * HD : (g + 1) * HD]
        s = lax.dot_general(
            q, k_all[...], (((1,), (1,)), ((), ())), preferred_element_type=jnp.float32
        )
        far = s[:, :listed]
        prior = jnp.where(has_prior, s[:, listed : listed + QB], NEG_FILL)
        own = jnp.where(causal, s[:, listed + QB :], NEG_FILL)
        s = jnp.concatenate([far, prior, own], axis=1)
        top = jnp.max(s, axis=1, keepdims=True)
        e = jnp.exp((s - top) * scale)
        total = jnp.sum(e, axis=1, keepdims=True)
        o = jnp.dot(e.astype(jnp.bfloat16), v_all[...], preferred_element_type=jnp.float32)
        out[:, g * HD : (g + 1) * HD] = (o / total).astype(jnp.bfloat16)


def attend(slots, info, q_rows, tiles, k_rows, v_rows, k_prior, v_prior, first):
    rows = q_rows.shape[0]
    blocks = rows // QB
    shards, heads = tiles.shape[:2]
    wide = GROUP * HD
    keys = (SEL + 2) * TILE
    return pl.pallas_call(
        functools.partial(attend_kernel, first),
        out_shape=jax.ShapeDtypeStruct((rows, heads * wide), jnp.bfloat16),
        grid_spec=pltpu.PrefetchScalarGridSpec(
            num_scalar_prefetch=2,
            grid=(heads, blocks),
            in_specs=[
                pl.BlockSpec((QB, wide), lambda h, b, *_: (b, first + h)),
                pl.BlockSpec(
                    (shards, 1, RANKS, 2, TILE, HD), lambda h, b, *_: (0, h, 0, 0, 0, 0)
                ),
                pl.BlockSpec((rows, HD), lambda h, b, *_: (0, first + h)),
                pl.BlockSpec((rows, HD), lambda h, b, *_: (0, first + h)),
                pl.BlockSpec((QB, HD), lambda h, b, *_: (0, first + h)),
                pl.BlockSpec((QB, HD), lambda h, b, *_: (0, first + h)),
            ],
            out_specs=pl.BlockSpec((QB, wide), lambda h, b, *_: (b, h)),
            scratch_shapes=[pltpu.VMEM((keys, HD), jnp.bfloat16)] * 2,
        ),
        compiler_params=pltpu.CompilerParams(vmem_limit_bytes=VMEM_LIMIT),
        cost_estimate=pl.CostEstimate(
            flops=4 * heads * rows * GROUP * keys * HD,
            bytes_accessed=2 * math.prod(tiles.shape),
            transcendentals=heads * rows * GROUP * keys,
        ),
        name="attend",
    )(slots, info, q_rows, tiles, k_rows, v_rows, k_prior, v_prior)


def on_device(queries, new_keys, new_values, cache_keys, cache_values, tile_lists):
    shards = lax.axis_size("seq")
    n_head = lax.axis_size("head")
    shard = lax.axis_index("seq")
    me = lax.axis_index("head")
    blocks, kv_here, _ = tile_lists.shape
    tiles_here = cache_keys.shape[0] // TILE

    listed = jnp.transpose(tile_lists, (1, 0, 2)).reshape(kv_here, blocks * SEL)
    local = listed % tiles_here
    match = (listed // tiles_here)[None] == jnp.arange(shards)[:, None, None]
    low = jnp.min(jnp.where(match, local[None], tiles_here - 1), axis=2)
    high = jnp.max(jnp.where(match, local[None], 0), axis=2)
    wanted = jnp.stack([low, high], axis=2).reshape(shards, kv_here * RANKS)
    asked = lax.all_to_all(wanted, "seq", split_axis=0, concat_axis=0, tiled=True)
    rank = jnp.any(match & (local[None] != low[:, :, None]), axis=0)
    slots = (listed // tiles_here * RANKS + rank).reshape(-1)
    info = jnp.reshape(shard, (1,))

    cut = max(1, kv_here - 1)
    parts = [(0, cut), (cut, kv_here - cut)] if kv_here > 1 else [(0, 1)]
    got = []
    for first, heads in parts:
        sent = gather_tiles(asked, cache_keys, cache_values, first, heads)
        got.append(lax.all_to_all(sent, "seq", split_axis=0, concat_axis=0, tiled=True))

    q_rows = swap_heads(queries, n_head, me)
    k_rows = swap_heads(new_keys, n_head, me)
    v_rows = swap_heads(new_values, n_head, me)
    route = [(i, i + 1) for i in range(shards - 1)]
    k_prior, v_prior = lax.ppermute((k_rows[-QB:], v_rows[-QB:]), "seq", route)

    outs = [
        attend(slots, info, q_rows, tiles, k_rows, v_rows, k_prior, v_prior, first)
        for (first, _), tiles in zip(parts, got)
    ]
    return swap_back(outs, n_head, me)


def solution(mesh):
    return jax.shard_map(
        on_device,
        mesh=mesh,
        in_specs=(
            P(("seq", "head"), None),
            P(("seq", "head"), None),
            P(("seq", "head"), None),
            P("seq", "head"),
            P("seq", "head"),
            P("seq", "head", None),
        ),
        out_specs=P(("seq", "head"), None),
        check_vma=False,
    )
```

time: 455 us -> 465 us (1.022)
  Pallas kernels: 0 us -> 299 us
  other arithmetic: 123 us -> 5.06 us
  local copies, waits for them, and re-layouts: 83.9 us -> 12.5 us
  matrix products: 46.8 us -> 0 us
  blocking collectives: 52.6 us -> 13.7 us
  loops' own time: 23.4 us -> 0 us
  waiting for transfers between devices: 75.1 us -> 91.4 us
    pallas_call x0 -> x4, Pallas kernels: none -> 299 us  [the longest x2 258 us: gather_tiles(): pl.pallas_call(functools.partial(gather_kernel, first, heads), out_shape=...]
    sub x4 -> x0, other arithmetic: 82.2 us -> none  [block_weights(): exponent = jnp.exp(masked - row_top)]
    dot_general x8 -> x0, matrix products: 46.8 us -> none  [the longest x4 29.1 us: block_weights(): jnp.einsum('qhgd,hkd->hgqk', query_block, all_keys, preferred_element_typ...]
    ppermute x2 -> x7, waiting for transfers between devices: 0.01 us -> 42.7 us  [the longest x3 28 us: swap_heads(): got = lax.ppermute(sent, 'head', [(0, 1), (1, 0)])]
    gather x10 -> x0, local copies, waits for them, and re-layouts: 34.4 us -> none  [the longest x8 26.7 us: remote_part(): received[block_owners, head_rows, block_ranks]]
    reduce_sum x7 -> x0, other arithmetic: 26.7 us -> none  [the longest x4 23.9 us: block_weights(): row_total = jnp.sum(exponent, axis=3)]
    all_to_all x5 -> x2, waiting for transfers between devices: 75.1 us -> 48.7 us  [on_device(): lax.all_to_all(sent, 'seq', split_axis=0, concat_axis=0, tiled=True)]
    another operation x2 -> x0, loops' own time: 23.4 us -> none  [the longest x1 13.1 us: on_device(): lax.map(lambda block_index: block_weights(block_index, got_keys), block_ids)]
  transfers between devices with their start and end apart: 7 -> 9, of which waited for: 2 -> 5; matrix products, arithmetic and copies ran while one was open for 43% -> 2% of each run, Pallas kernels for 0% -> 23%
where the time goes in v1:
time: 465 us
  Pallas kernels  299 us (64%)
  waiting for transfers between devices  91.4 us (20%)
  starting transfers between devices  43.3 us (9%)
  blocking collectives  13.7 us (3%)
  local copies, waits for them, and re-layouts  12.5 us (3%)
  other arithmetic  5.06 us (1%)
    pallas_call x2, Pallas kernels, gather_tiles(): pl.pallas_call(functools.partial(gather_kernel, first, heads), out_shape=...  258 us
    all_to_all x2, waiting for transfers between devices, on_device(): lax.all_to_all(sent, 'seq', split_axis=0, concat_axis=0, tiled=True)  48.7 us
    pallas_call x2, Pallas kernels, attend(): pl.pallas_call(functools.partial(attend_kernel, first), out_shape=jax.Sha...  40.8 us
    all_to_all x2, starting transfers between devices, on_device(): lax.all_to_all(sent, 'seq', split_axis=0, concat_axis=0, tiled=True)  32.7 us
    ppermute x3, waiting for transfers between devices, swap_heads(): got = lax.ppermute(sent, 'head', [(0, 1), (1, 0)])  28 us
    ppermute x2, waiting for transfers between devices, swap_back(): got = lax.ppermute(sent, 'head', [(0, 1), (1, 0)])  14.7 us
    all_to_all x1, blocking collectives, on_device(): lax.all_to_all(wanted, 'seq', split_axis=0, concat_axis=0, tiled=True)  13.7 us
  transfers between devices with their start and end apart: 9, of which 5 were waited for; matrix products, arithmetic and copies ran while one was open for 2% of the time, Pallas kernels for 23%

profile of v1, /device:TPU:0, one launch (start us, length us, event | category | flops | bytes accessed | tf_op | source)
XLA Modules:
  0.0 464.8 jit_solution(10469712392572287859)
XLA Ops:
  0.0 0.7 copy.25
  0.7 0.1 reshape.68
  0.8 0.2 select_reduce_fusion
  1.0 0.1 copy.28
  1.1 13.7 %all_to_all.21 = s32[16,1,8]{2,1,0:T(1,128)} all-to-all(s32[16,1,8]{2,1,0:T(1,128)S(1)} %copy.28), channel_id=1, replica_groups=mesh['seq'=16,'head'=2] {'seq'}, dimensions={0} | all-to-all | bytes 1024 | tf_op jit(solution)/shard_map/all_to_all | solution.py:190
  14.8 192.5 %gather_tiles.2 = bf16[16,3,2,2,128,128]{5,4,3,2,1,0:T(8,128)(2,1)} custom-call(s32[16,8]{1,0:T(8,128)} %bitcast.6, bf16[2048,512]{1,0:T(8,128)(2,1)} %keys.3, bf16[2048,512]{1,0:T(8,128)(2,1)} %values.3), custom_call_target="tpu_custom_call" | custom-call | bytes 12582912 | tf_op jit(solution)/shard_map/gather_tiles/pallas_call | solution.py:75
  207.3 4.6 all-to-all-start.1
  211.9 65.4 %gather_tiles.3 = bf16[16,1,2,2,128,128]{5,4,3,2,1,0:T(8,128)(2,1)} custom-call(s32[16,8]{1,0:T(8,128)} %bitcast.7, bf16[2048,512]{1,0:T(8,128)(2,1)} %keys.3, bf16[2048,512]{1,0:T(8,128)(2,1)} %values.3), custom_call_target="tpu_custom_call" | custom-call | bytes 4194304 | tf_op jit(solution)/shard_map/gather_tiles/pallas_call | solution.py:75
  277.4 48.7 %all-to-all-done.1.tiles = bf16[16,3,2,2,128,128]{5,4,3,2,1,0:T(8,128)(2,1)} async-done(((bf16[16,3,2,2,128,128]{5,4,3,2,1,0:T(8,128)(2,1)}), bf16[16,3,2,2,128,128]{5,4,3,2,1,0:T(8,128)(2,1)}, u32[]{:S(2)}, u32[]{:S(2)}) %all-to-all-start.1) | async-done | bytes 6291488 | tf_op jit(solution)/shard_map/all_to_all | solution.py:200
  326.1 28.1 %all-to-all-start.2 = ((bf16[16,1,2,2,128,128]{5,4,3,2,1,0:T(8,128)(2,1)}), bf16[16,1,2,2,128,128]{5,4,3,2,1,0:T(8,128)(2,1)}, u32[]{:S(2)}, u32[]{:S(2)}) async-start(bf16[16,1,2,2,128,128]{5,4,3,2,1,0:T(8,128)(2,1)} %gather_tiles.3), calls=%async_computation.2 | async-start | bytes 4194304 | tf_op jit(solution)/shard_map/all_to_all | solution.py:200
  354.2 0.0 copy-start.2
  354.2 2.8 constant_dynamic-slice_fusion.7
  356.9 1.5 collective-permute-start
  358.5 0.0 copy-done.2
  358.5 0.8 constant_dynamic-slice_fusion.5
  359.2 0.5 collective-permute-start.1
  359.7 1.1 constant_dynamic-slice_fusion.3
  360.8 1.6 collective-permute-start.2
  362.4 0.1 fusion.1
  362.5 0.1 reshape.67
  362.6 0.1 reshape.70
  362.7 26.1 %collective-permute-done.1 = bf16[256,512]{1,0:T(8,128)(2,1)S(1)} collective-permute-done((bf16[256,512]{1,0:T(8,128)(2,1)}, bf16[256,512]{1,0:T(8,128)(2,1)S(1)}, u32[]{:S(2)}, u32[]{:S(2)}) %collective-permute-start.1) | collective-permute-done | bytes 262176 | tf_op jit(solution)/shard_map/ppermute | solution.py:29
  388.8 0.0 copy-start.3
  388.8 0.7 copy-done.3
  389.5 1.2 maximum_select_fusion.1.k_rows
  390.7 1.3 collective-permute-start.3
  392.0 1.9 collective-permute-done.2
  393.9 1.2 maximum_select_fusion.2.v_rows
  395.1 2.6 collective-permute-start.4
  397.7 0.0 collective-permute-done
  397.7 2.4 maximum_select_fusion.q_ref
  400.1 0.0 collective-permute-done.3.k_prior
  400.1 0.0 collective-permute-done.4.v_prior
  400.1 29.6 %attend.2 = bf16[512,1536]{1,0:T(8,128)(2,1)S(1)} custom-call(s32[192]{0:T(256)S(1)} %multiply_add_fusion.slots, s32[1]{0:T(128)} %bitcast.1.info, bf16[512,2048]{1,0:T(8,128)(2,1)} %maximum_select_fusion.q_ref, bf16[16,3,2,2,128,128]{5,4,3,2,1,0:T(8,128)(2,1)} %all-to-all-done.1.tiles, bf16[512,512]{1,0:T(8,128)(2,1)S(1)} %maximum_select_fusion.1.k_rows, ...), custom_call_target="tpu_custom_call" | custom-call | flops 5637144576 | bytes 6291456 | tf_op jit(solution)/shard_map/attend/pallas_call | solution.py:147
  429.7 0.2 broadcast_in_dim.27
  429.9 0.0 copy-start
  430.0 1.0 constant_dynamic-slice_fusion.1
  431.0 0.0 copy-start.1
  431.0 1.3 copy-done.1
  432.3 1.5 collective-permute-start.5
  433.8 0.0 all-to-all-done.2.tiles
  433.8 0.0 copy-done
  433.8 11.1 %attend.3 = bf16[512,512]{1,0:T(8,128)(2,1)S(1)} custom-call(s32[192]{0:T(256)S(1)} %multiply_add_fusion.slots, s32[1]{0:T(128)} %bitcast.1.info, bf16[512,2048]{1,0:T(8,128)(2,1)S(1)} %copy-done, bf16[16,1,2,2,128,128]{5,4,3,2,1,0:T(8,128)(2,1)} %all-to-all-done.2.tiles, bf16[512,512]{1,0:T(8,128)(2,1)S(1)} %maximum_select_fusion.1.k_rows, ...), custom_call_target="tpu_custom_call" | custom-call | flops 1879048192 | bytes 2097152 | tf_op jit(solution)/shard_map/attend/pallas_call | solution.py:147
  445.0 7.9 %collective-permute-done.5 = bf16[256,1536]{1,0:T(8,128)(2,1)} collective-permute-done((bf16[256,1536]{1,0:T(8,128)(2,1)}, bf16[256,1536]{1,0:T(8,128)(2,1)}, u32[]{:S(2)}, u32[]{:S(2)}) %collective-permute-start.5) | collective-permute-done | bytes 786464 | tf_op jit(solution)/shard_map/ppermute | solution.py:46
  452.9 2.1 constant_dynamic-update-slice_fusion.1
  455.0 0.7 constant_dynamic-slice_fusion
  455.7 1.5 collective-permute-start.6
  457.3 6.8 %collective-permute-done.6 = bf16[256,512]{1,0:T(8,128)(2,1)S(1)} collective-permute-done((bf16[256,512]{1,0:T(8,128)(2,1)S(1)}, bf16[256,512]{1,0:T(8,128)(2,1)S(1)}, u32[]{:S(2)}, u32[]{:S(2)}) %collective-permute-start.6) | collective-permute-done | bytes 262176 | tf_op jit(solution)/shard_map/ppermute | solution.py:46
  464.1 0.7 constant_dynamic-update-slice_fusion
  (7 shorter events, 0.1 us)
Async XLA Ops:
  207.3 118.8 %all-to-all-start.1 = ((bf16[16,3,2,2,128,128]{5,4,3,2,1,0:T(8,128)(2,1)}), bf16[16,3,2,2,128,128]{5,4,3,2,1,0:T(8,128)(2,1)}, u32[]{:S(2)}, u32[]{:S(2)}) async-start(bf16[16,3,2,2,128,128]{5,4,3,2,1,0:T(8,128)(2,1)} %gather_tiles.2), calls=%async_computation.1 | async-start | bytes 12582912 | tf_op jit(solution)/shard_map/all_to_all | solution.py:200
  326.1 107.8 %all-to-all-start.2 = ((bf16[16,1,2,2,128,128]{5,4,3,2,1,0:T(8,128)(2,1)}), bf16[16,1,2,2,128,128]{5,4,3,2,1,0:T(8,128)(2,1)}, u32[]{:S(2)}, u32[]{:S(2)}) async-start(bf16[16,1,2,2,128,128]{5,4,3,2,1,0:T(8,128)(2,1)} %gather_tiles.3), calls=%async_computation.2 | async-start | bytes 4194304 | tf_op jit(solution)/shard_map/all_to_all | solution.py:200
  354.2 4.3 copy-start.2
  356.9 40.8 %collective-permute-start = (bf16[256,2048]{1,0:T(8,128)(2,1)}, bf16[256,2048]{1,0:T(8,128)(2,1)S(1)}, u32[]{:S(2)}, u32[]{:S(2)}) collective-permute-start(bf16[256,2048]{1,0:T(8,128)(2,1)} %get-tuple-element.8), channel_id=1, source_target_pairs={{0,1},{1,0},{2,3},{3,2},{4,5},{5,4},{6,7},{7,6},{8,9},{9,8},{10,11... | collective-permute-start | bytes 3145736 | tf_op jit(solution)/shard_map/ppermute | solution.py:29
  359.2 29.5 %collective-permute-start.1 = (bf16[256,512]{1,0:T(8,128)(2,1)}, bf16[256,512]{1,0:T(8,128)(2,1)S(1)}, u32[]{:S(2)}, u32[]{:S(2)}) collective-permute-start(bf16[256,512]{1,0:T(8,128)(2,1)} %get-tuple-element.16), channel_id=1, source_target_pairs={{0,1},{1,0},{2,3},{3,2},{4,5},{5,4},{6,7},{7,6},{8,9},{9,8},{10,11... | collective-permute-start | bytes 786440 | tf_op jit(solution)/shard_map/ppermute | solution.py:29
  360.8 33.1 %collective-permute-start.2 = (bf16[256,512]{1,0:T(8,128)(2,1)S(1)}, bf16[256,512]{1,0:T(8,128)(2,1)}, u32[]{:S(2)}, u32[]{:S(2)}) collective-permute-start(bf16[256,512]{1,0:T(8,128)(2,1)S(1)} %get-tuple-element.14), channel_id=1, source_target_pairs={{0,1},{1,0},{2,3},{3,2},{4,5},{5,4},{6,7},{7,6},{8,9},{9,8},{10,11... | collective-permute-start | bytes 786440 | tf_op jit(solution)/shard_map/ppermute | solution.py:29
  388.8 0.7 copy-start.3
  390.7 9.4 %collective-permute-start.3 = (bf16[128,512]{1,0:T(8,128)(2,1)S(1)}, bf16[128,512]{1,0:T(8,128)(2,1)S(1)}, u32[]{:S(2)}, u32[]{:S(2)}) collective-permute-start(bf16[128,512]{1,0:T(8,128)(2,1)S(1)} %slice.8), channel_id=1, source_target_pairs={{0,2},{2,4},{4,6},{6,8},{8,10},{10,12},{12,14},{14,16},{16,18},{18... | collective-permute-start | bytes 393224 | tf_op jit(solution)/shard_map/ppermute | solution.py:206
  395.1 5.0 %collective-permute-start.4 = (bf16[128,512]{1,0:T(8,128)(2,1)S(1)}, bf16[128,512]{1,0:T(8,128)(2,1)S(1)}, u32[]{:S(2)}, u32[]{:S(2)}) collective-permute-start(bf16[128,512]{1,0:T(8,128)(2,1)S(1)} %slice.9), channel_id=1, source_target_pairs={{0,2},{2,4},{4,6},{6,8},{8,10},{10,12},{12,14},{14,16},{16,18},{18... | collective-permute-start | bytes 393224 | tf_op jit(solution)/shard_map/ppermute | solution.py:206
  429.9 3.9 copy-start
  431.0 1.3 copy-start.1
  432.3 20.6 %collective-permute-start.5 = (bf16[256,1536]{1,0:T(8,128)(2,1)}, bf16[256,1536]{1,0:T(8,128)(2,1)}, u32[]{:S(2)}, u32[]{:S(2)}) collective-permute-start(bf16[256,1536]{1,0:T(8,128)(2,1)} %get-tuple-element.9), channel_id=1, source_target_pairs={{0,1},{1,0},{2,3},{3,2},{4,5},{5,4},{6,7},{7,6},{8,9},{9,8},{10,11... | collective-permute-start | bytes 2359304 | tf_op jit(solution)/shard_map/ppermute | solution.py:46
  455.7 8.3 %collective-permute-start.6 = (bf16[256,512]{1,0:T(8,128)(2,1)S(1)}, bf16[256,512]{1,0:T(8,128)(2,1)S(1)}, u32[]{:S(2)}, u32[]{:S(2)}) collective-permute-start(bf16[256,512]{1,0:T(8,128)(2,1)S(1)} %get-tuple-element.11), channel_id=1, source_target_pairs={{0,1},{1,0},{2,3},{3,2},{4,5},{5,4},{6,7},{7,6},{8,9},{9,8},{10,11... | collective-permute-start | bytes 786440 | tf_op jit(solution)/shard_map/ppermute | solution.py:46

commit v2 on v1

--- a/solution.py
+++ b/solution.py
@@ -50,22 +50,32 @@
     return result
 
 
-def gather_kernel(first, heads, asked, keys, values, out, sem):
+def gather_kernel(first, heads, asked, keys, values, out, held, load_sem, sem):
     shards = out.shape[0]
-
-    def one(i, carry):
-        peer = i // (heads * RANKS)
-        rest = i % (heads * RANKS)
-        head = rest // RANKS
-        rank = rest % RANKS
-        tile = asked[peer, (first + head) * RANKS + rank]
-        rows = pl.ds(pl.multiple_of(tile * TILE, TILE), TILE)
-        cols = pl.ds(pl.multiple_of((first + head) * HD, HD), HD)
-        pltpu.make_async_copy(keys.at[rows, cols], out.at[peer, head, rank, 0], sem).start()
-        pltpu.make_async_copy(values.at[rows, cols], out.at[peer, head, rank, 1], sem).start()
-        return carry
-
-    lax.fori_loop(0, shards * heads * RANKS, one, 0)
+    loads = []
+    for head in range(heads):
+        cols = pl.ds((first + head) * HD, HD)
+        for kind, source in enumerate((keys, values)):
+            load = pltpu.make_async_copy(
+                source.at[:, cols], held.at[head, kind], load_sem.at[head, kind]
+            )
+            load.start()
+            loads.append(load)
+    for head in range(heads):
+        loads[2 * head].wait()
+        loads[2 * head + 1].wait()
+
+        def one(i, carry, head=head):
+            peer = i // RANKS
+            rank = i % RANKS
+            tile = asked[peer, (first + head) * RANKS + rank]
+            rows = pl.ds(pl.multiple_of(tile * TILE, TILE), TILE)
+            pltpu.make_async_copy(
+                held.at[head, :, rows], out.at[peer, head, rank], sem
+            ).start()
+            return carry
+
+        lax.fori_loop(0, shards * RANKS, one, 0, unroll=4)
     pltpu.make_async_copy(out, out, sem).wait()
 
 
@@ -80,8 +90,13 @@
             grid=(),
             in_specs=[pl.BlockSpec(memory_space=pl.ANY)] * 2,
             out_specs=pl.BlockSpec(memory_space=pl.ANY),
-            scratch_shapes=[pltpu.SemaphoreType.DMA],
-        ),
+            scratch_shapes=[
+                pltpu.VMEM((heads, 2, keys.shape[0], HD), jnp.bfloat16),
+                pltpu.SemaphoreType.DMA((heads, 2)),
+                pltpu.SemaphoreType.DMA,
+            ],
+        ),
+        compiler_params=pltpu.CompilerParams(vmem_limit_bytes=VMEM_LIMIT),
         cost_estimate=pl.CostEstimate(
             flops=0, bytes_accessed=4 * math.prod(shape), transcendentals=0
         ),
@@ -192,18 +207,21 @@
     slots = (listed // tiles_here * RANKS + rank).reshape(-1)
     info = jnp.reshape(shard, (1,))
 
-    cut = max(1, kv_here - 1)
-    parts = [(0, cut), (cut, kv_here - cut)] if kv_here > 1 else [(0, 1)]
-    got = []
-    for first, heads in parts:
-        sent = gather_tiles(asked, cache_keys, cache_values, first, heads)
-        got.append(lax.all_to_all(sent, "seq", split_axis=0, concat_axis=0, tiled=True))
-
     q_rows = swap_heads(queries, n_head, me)
     k_rows = swap_heads(new_keys, n_head, me)
     v_rows = swap_heads(new_values, n_head, me)
     route = [(i, i + 1) for i in range(shards - 1)]
     k_prior, v_prior = lax.ppermute((k_rows[-QB:], v_rows[-QB:]), "seq", route)
+
+    cut = max(1, kv_here - 1)
+    parts = [(0, cut), (cut, kv_here - cut)] if kv_here > 1 else [(0, 1)]
+    sent = [gather_tiles(asked, cache_keys, cache_values, *part) for part in parts]
+    got = [lax.all_to_all(sent[0], "seq", split_axis=0, concat_axis=0, tiled=True)]
+    for later in sent[1:]:
+        later, q_rows, k_rows, v_rows, k_prior, v_prior = lax.optimization_barrier(
+            (later, q_rows, k_rows, v_rows, k_prior, v_prior)
+        )
+        got.append(lax.all_to_all(later, "seq", split_axis=0, concat_axis=0, tiled=True))
 
     outs = [
         attend(slots, info, q_rows, tiles, k_rows, v_rows, k_prior, v_prior, first)

time: 465 us -> 240 us (0.52)
  the two profiles are of different devices: /device:TPU:0 before, /device:TPU:10 now
where the time goes in v2:
time: 240 us
  waiting for transfers between devices  136 us (57%)
  Pallas kernels  48.5 us (20%)
  starting transfers between devices  25 us (10%)
  local copies, waits for them, and re-layouts  14.8 us (6%)
  blocking collectives  10.1 us (4%)
  other arithmetic  5 us (2%)
    all_to_all x1, waiting for transfers between devices, on_device(): lax.all_to_all(sent[0], 'seq', split_axis=0, concat_axis=0, tiled=True)  90.3 us
    pallas_call x2, Pallas kernels, attend(): pl.pallas_call(functools.partial(attend_kernel, first), out_shape=jax.Sha...  40.7 us
    ppermute x3, waiting for transfers between devices, swap_heads(): got = lax.ppermute(sent, 'head', [(0, 1), (1, 0)])  23.6 us
    all_to_all x1, waiting for transfers between devices, on_device(): lax.all_to_all(later, 'seq', split_axis=0, concat_axis=0, tiled=True)  13.3 us
    all_to_all x1, blocking collectives, on_device(): lax.all_to_all(wanted, 'seq', split_axis=0, concat_axis=0, tiled=True)  10.1 us
    pallas_call x2, Pallas kernels, gather_tiles(): pl.pallas_call(functools.partial(gather_kernel, first, heads), out_shape=...  7.74 us
    ppermute x2, waiting for transfers between devices, swap_back(): got = lax.ppermute(sent, 'head', [(0, 1), (1, 0)])  7.29 us
    all_to_all x1, starting transfers between devices, on_device(): lax.all_to_all(later, 'seq', split_axis=0, concat_axis=0, tiled=True)  7.25 us
  transfers between devices with their start and end apart: 9, of which 6 were waited for; matrix products, arithmetic and copies ran while one was open for 5% of the time, Pallas kernels for 18%

profile of v2, /device:TPU:10, one launch (start us, length us, event | category | flops | bytes accessed | tf_op | source)
XLA Modules:
  0.0 239.6 jit_solution(4306684104848965620)
XLA Ops:
  0.0 0.7 copy.25
  0.7 0.1 reshape.68
  0.8 0.2 select_reduce_fusion
  1.0 0.1 copy.28
  1.1 10.1 %all_to_all.21 = s32[16,1,8]{2,1,0:T(1,128)S(1)} all-to-all(s32[16,1,8]{2,1,0:T(1,128)S(1)} %copy.28), channel_id=1, replica_groups=mesh['seq'=16,'head'=2] {'seq'}, dimensions={0} | all-to-all | bytes 1024 | tf_op jit(solution)/shard_map/all_to_all | solution.py:205
  11.2 0.0 copy-start
  11.2 1.6 copy-done
  12.8 4.5 %gather_tiles.3 = bf16[16,3,2,2,128,128]{5,4,3,2,1,0:T(8,128)(2,1)} custom-call(s32[16,8]{1,0:T(8,128)S(1)} %bitcast.6, bf16[2048,512]{1,0:T(8,128)(2,1)S(1)} %copy-done, bf16[2048,512]{1,0:T(8,128)(2,1)} %values.3), custom_call_target="tpu_custom_call" | custom-call | bytes 12582912 | tf_op jit(solution)/shard_map/gather_tiles/pallas_call | solution.py:85
  17.3 6.8 %all-to-all-start.1 = ((bf16[16,3,2,2,128,128]{5,4,3,2,1,0:T(8,128)(2,1)}), bf16[16,3,2,2,128,128]{5,4,3,2,1,0:T(8,128)(2,1)}, u32[]{:S(2)}, u32[]{:S(2)}) async-start(bf16[16,3,2,2,128,128]{5,4,3,2,1,0:T(8,128)(2,1)} %gather_tiles.3), calls=%async_computation.1 | async-start | bytes 12582912 | tf_op jit(solution)/shard_map/all_to_all | solution.py:219
  24.2 0.0 copy-start.4
  24.2 2.8 %constant_dynamic-slice_fusion.7 = (bf16[256,2048]{1,0:T(8,128)(2,1)S(1)}, bf16[256,2048]{1,0:T(8,128)(2,1)}) fusion(bf16[256,4096]{1,0:T(8,128)(2,1)} %param.6, s32[]{:T(128)S(6)} %select_n.87, s32[]{:T(128)S(6)} %select_n.88), kind=kLoop, calls=%fused_computation.20 | loop fusion | bytes 4194312 | tf_op jit(solution)/shard_map/dynamic_slice | solution.py:27
  26.9 1.5 collective-permute-start
  28.5 0.0 copy-done.4
  28.5 0.7 constant_dynamic-slice_fusion.5
  29.2 0.5 collective-permute-start.1
  29.7 1.8 constant_dynamic-slice_fusion.3
  31.5 1.5 collective-permute-start.2
  33.0 0.0 copy-start.3
  33.0 3.2 %gather_tiles.2 = bf16[16,1,2,2,128,128]{5,4,3,2,1,0:T(8,128)(2,1)} custom-call(s32[16,8]{1,0:T(8,128)S(1)} %bitcast.7, bf16[2048,512]{1,0:T(8,128)(2,1)} %keys.3, bf16[2048,512]{1,0:T(8,128)(2,1)} %values.3), custom_call_target="tpu_custom_call" | custom-call | bytes 4194304 | tf_op jit(solution)/shard_map/gather_tiles/pallas_call | solution.py:85
  36.2 22.5 %collective-permute-done.1 = bf16[256,512]{1,0:T(8,128)(2,1)S(1)} collective-permute-done((bf16[256,512]{1,0:T(8,128)(2,1)}, bf16[256,512]{1,0:T(8,128)(2,1)S(1)}, u32[]{:S(2)}, u32[]{:S(2)}) %collective-permute-start.1) | collective-permute-done | bytes 262176 | tf_op jit(solution)/shard_map/ppermute | solution.py:29
  58.8 0.0 copy-start.5
  58.8 0.7 copy-done.5
  59.5 1.2 maximum_select_fusion.1.k_rows
  60.7 1.9 collective-permute-start.3
  62.6 1.1 collective-permute-done.2
  63.7 0.0 copy-done.3
  63.7 1.2 maximum_select_fusion.2.v_rows
  64.9 2.4 collective-permute-start.4
  67.3 0.0 collective-permute-done
  67.3 2.3 maximum_select_fusion.q_ref
  69.6 0.0 collective-permute-done.3.k_prior
  69.6 1.6 collective-permute-done.4.v_prior
  71.2 90.3 %all-to-all-done.1.tiles = bf16[16,3,2,2,128,128]{5,4,3,2,1,0:T(8,128)(2,1)} async-done(((bf16[16,3,2,2,128,128]{5,4,3,2,1,0:T(8,128)(2,1)}), bf16[16,3,2,2,128,128]{5,4,3,2,1,0:T(8,128)(2,1)}, u32[]{:S(2)}, u32[]{:S(2)}) %all-to-all-start.1) | async-done | bytes 6291488 | tf_op jit(solution)/shard_map/all_to_all | solution.py:219
  161.5 7.2 %all-to-all-start.2 = ((bf16[16,1,2,2,128,128]{5,4,3,2,1,0:T(8,128)(2,1)}), bf16[16,1,2,2,128,128]{5,4,3,2,1,0:T(8,128)(2,1)}, u32[]{:S(2)}, u32[]{:S(2)}) async-start(bf16[16,1,2,2,128,128]{5,4,3,2,1,0:T(8,128)(2,1)} %gather_tiles.2), calls=%async_computation.2 | async-start | bytes 4194304 | tf_op jit(solution)/shard_map/all_to_all | solution.py:224
  168.7 0.1 reshape.67
  168.8 0.1 fusion.1
  168.9 0.1 reshape.70
  169.0 29.6 %attend.2 = bf16[512,1536]{1,0:T(8,128)(2,1)S(1)} custom-call(s32[192]{0:T(256)S(1)} %multiply_add_fusion.slots, s32[1]{0:T(128)} %bitcast.1.info, bf16[512,2048]{1,0:T(8,128)(2,1)} %maximum_select_fusion.q_ref, bf16[16,3,2,2,128,128]{5,4,3,2,1,0:T(8,128)(2,1)} %all-to-all-done.1.tiles, bf16[512,512]{1,0:T(8,128)(2,1)S(1)} %maximum_select_fusion.1.k_rows, ...), custom_call_target="tpu_custom_call" | custom-call | flops 5637144576 | bytes 6291456 | tf_op jit(solution)/shard_map/attend/pallas_call | solution.py:162
  198.6 0.2 broadcast_in_dim.27
  198.9 0.0 copy-start.1
  198.9 1.1 constant_dynamic-slice_fusion.1
  200.0 0.0 copy-start.2
  200.0 1.3 copy-done.2
  201.3 1.5 collective-permute-start.5
  202.8 13.3 %all-to-all-done.2.tiles = bf16[16,1,2,2,128,128]{5,4,3,2,1,0:T(8,128)(2,1)} async-done(((bf16[16,1,2,2,128,128]{5,4,3,2,1,0:T(8,128)(2,1)}), bf16[16,1,2,2,128,128]{5,4,3,2,1,0:T(8,128)(2,1)}, u32[]{:S(2)}, u32[]{:S(2)}) %all-to-all-start.2) | async-done | bytes 2097184 | tf_op jit(solution)/shard_map/all_to_all | solution.py:224
  216.1 0.0 copy-done.1
  216.1 11.1 %attend.3 = bf16[512,512]{1,0:T(8,128)(2,1)S(1)} custom-call(s32[192]{0:T(256)S(1)} %multiply_add_fusion.slots, s32[1]{0:T(128)} %bitcast.1.info, bf16[512,2048]{1,0:T(8,128)(2,1)S(1)} %copy-done.1, bf16[16,1,2,2,128,128]{5,4,3,2,1,0:T(8,128)(2,1)} %all-to-all-done.2.tiles, bf16[512,512]{1,0:T(8,128)(2,1)S(1)} %maximum_select_fusion.1.k_rows, ...), custom_call_target="tpu_custom_call" | custom-call | flops 1879048192 | bytes 2097152 | tf_op jit(solution)/shard_map/attend/pallas_call | solution.py:162
  227.2 0.0 collective-permute-done.5
  227.3 2.1 constant_dynamic-update-slice_fusion.1
  229.3 0.7 constant_dynamic-slice_fusion
  230.1 1.5 collective-permute-start.6
  231.6 7.3 %collective-permute-done.6 = bf16[256,512]{1,0:T(8,128)(2,1)S(1)} collective-permute-done((bf16[256,512]{1,0:T(8,128)(2,1)S(1)}, bf16[256,512]{1,0:T(8,128)(2,1)S(1)}, u32[]{:S(2)}, u32[]{:S(2)}) %collective-permute-start.6) | collective-permute-done | bytes 262176 | tf_op jit(solution)/shard_map/ppermute | solution.py:46
  238.9 0.7 constant_dynamic-update-slice_fusion
  (7 shorter events, 0.1 us)
Async XLA Ops:
  11.2 1.6 copy-start
  17.3 144.1 %all-to-all-start.1 = ((bf16[16,3,2,2,128,128]{5,4,3,2,1,0:T(8,128)(2,1)}), bf16[16,3,2,2,128,128]{5,4,3,2,1,0:T(8,128)(2,1)}, u32[]{:S(2)}, u32[]{:S(2)}) async-start(bf16[16,3,2,2,128,128]{5,4,3,2,1,0:T(8,128)(2,1)} %gather_tiles.3), calls=%async_computation.1 | async-start | bytes 12582912 | tf_op jit(solution)/shard_map/all_to_all | solution.py:219
  24.2 4.3 %copy-start.4 = (bf16[256,1024]{1,0:T(8,128)(2,1)S(1)}, bf16[256,1024]{1,0:T(8,128)(2,1)}, u32[]{:S(2)}) copy-start(bf16[256,1024]{1,0:T(8,128)(2,1)} %param.7) | copy-start | bytes 1572868
  26.9 40.4 %collective-permute-start = (bf16[256,2048]{1,0:T(8,128)(2,1)}, bf16[256,2048]{1,0:T(8,128)(2,1)S(1)}, u32[]{:S(2)}, u32[]{:S(2)}) collective-permute-start(bf16[256,2048]{1,0:T(8,128)(2,1)} %get-tuple-element.20), channel_id=1, source_target_pairs={{0,1},{1,0},{2,3},{3,2},{4,5},{5,4},{6,7},{7,6},{8,9},{9,8},{10,11... | collective-permute-start | bytes 3145736 | tf_op jit(solution)/shard_map/ppermute | solution.py:29
  29.2 29.6 %collective-permute-start.1 = (bf16[256,512]{1,0:T(8,128)(2,1)}, bf16[256,512]{1,0:T(8,128)(2,1)S(1)}, u32[]{:S(2)}, u32[]{:S(2)}) collective-permute-start(bf16[256,512]{1,0:T(8,128)(2,1)} %get-tuple-element.28), channel_id=1, source_target_pairs={{0,1},{1,0},{2,3},{3,2},{4,5},{5,4},{6,7},{7,6},{8,9},{9,8},{10,11... | collective-permute-start | bytes 786440 | tf_op jit(solution)/shard_map/ppermute | solution.py:29
  31.5 32.2 %collective-permute-start.2 = (bf16[256,512]{1,0:T(8,128)(2,1)S(1)}, bf16[256,512]{1,0:T(8,128)(2,1)}, u32[]{:S(2)}, u32[]{:S(2)}) collective-permute-start(bf16[256,512]{1,0:T(8,128)(2,1)S(1)} %get-tuple-element.26), channel_id=1, source_target_pairs={{0,1},{1,0},{2,3},{3,2},{4,5},{5,4},{6,7},{7,6},{8,9},{9,8},{10,11... | collective-permute-start | bytes 786440 | tf_op jit(solution)/shard_map/ppermute | solution.py:29
  33.0 30.7 %copy-start.3 = (bf16[256,512]{1,0:T(8,128)(2,1)S(1)}, bf16[256,512]{1,0:T(8,128)(2,1)}, u32[]{:S(2)}) copy-start(bf16[256,512]{1,0:T(8,128)(2,1)} %get-tuple-element.25) | copy-start | bytes 786436
  58.8 0.7 copy-start.5
  60.7 9.0 %collective-permute-start.3 = (bf16[128,512]{1,0:T(8,128)(2,1)S(1)}, bf16[128,512]{1,0:T(8,128)(2,1)S(1)}, u32[]{:S(2)}, u32[]{:S(2)}) collective-permute-start(bf16[128,512]{1,0:T(8,128)(2,1)S(1)} %slice.8), channel_id=1, source_target_pairs={{0,2},{2,4},{4,6},{6,8},{8,10},{10,12},{12,14},{14,16},{16,18},{18... | collective-permute-start | bytes 393224 | tf_op jit(solution)/shard_map/ppermute | solution.py:214
  64.9 6.3 %collective-permute-start.4 = (bf16[128,512]{1,0:T(8,128)(2,1)S(1)}, bf16[128,512]{1,0:T(8,128)(2,1)S(1)}, u32[]{:S(2)}, u32[]{:S(2)}) collective-permute-start(bf16[128,512]{1,0:T(8,128)(2,1)S(1)} %slice.9), channel_id=1, source_target_pairs={{0,2},{2,4},{4,6},{6,8},{8,10},{10,12},{12,14},{14,16},{16,18},{18... | collective-permute-start | bytes 393224 | tf_op jit(solution)/shard_map/ppermute | solution.py:214
  161.5 54.6 %all-to-all-start.2 = ((bf16[16,1,2,2,128,128]{5,4,3,2,1,0:T(8,128)(2,1)}), bf16[16,1,2,2,128,128]{5,4,3,2,1,0:T(8,128)(2,1)}, u32[]{:S(2)}, u32[]{:S(2)}) async-start(bf16[16,1,2,2,128,128]{5,4,3,2,1,0:T(8,128)(2,1)} %gather_tiles.2), calls=%async_computation.2 | async-start | bytes 4194304 | tf_op jit(solution)/shard_map/all_to_all | solution.py:224
  198.9 17.2 %copy-start.1 = (bf16[512,2048]{1,0:T(8,128)(2,1)S(1)}, bf16[512,2048]{1,0:T(8,128)(2,1)}, u32[]{:S(2)}) copy-start(bf16[512,2048]{1,0:T(8,128)(2,1)} %maximum_select_fusion.q_ref) | copy-start | bytes 6291460
  200.0 1.3 copy-start.2
  201.3 25.9 %collective-permute-start.5 = (bf16[256,1536]{1,0:T(8,128)(2,1)}, bf16[256,1536]{1,0:T(8,128)(2,1)}, u32[]{:S(2)}, u32[]{:S(2)}) collective-permute-start(bf16[256,1536]{1,0:T(8,128)(2,1)} %get-tuple-element.21), channel_id=1, source_target_pairs={{0,1},{1,0},{2,3},{3,2},{4,5},{5,4},{6,7},{7,6},{8,9},{9,8},{10,11... | collective-permute-start | bytes 2359304 | tf_op jit(solution)/shard_map/ppermute | solution.py:46
  230.1 8.8 %collective-permute-start.6 = (bf16[256,512]{1,0:T(8,128)(2,1)S(1)}, bf16[256,512]{1,0:T(8,128)(2,1)S(1)}, u32[]{:S(2)}, u32[]{:S(2)}) collective-permute-start(bf16[256,512]{1,0:T(8,128)(2,1)S(1)} %get-tuple-element.23), channel_id=1, source_target_pairs={{0,1},{1,0},{2,3},{3,2},{4,5},{5,4},{6,7},{7,6},{8,9},{9,8},{10,11... | collective-permute-start | bytes 786440 | tf_op jit(solution)/shard_map/ppermute | solution.py:46

commit v3 on v2

v3 whole, which is shorter than its diff:
```python
import functools
import math

import jax
import jax.numpy as jnp
from jax import lax
from jax.experimental import pallas as pl
from jax.experimental.pallas import tpu as pltpu
from jax.sharding import PartitionSpec as P

HQ = 32
KV = 8
HD = 128
QB = 128
TILE = 128
SEL = 12
RANKS = 2
GROUP = HQ // KV
NEG_FILL = -1e30
VMEM_LIMIT = 50 * 1024 * 1024

PLACES = 8
CUTS = (4, 6, 7)
HAND = 3
RELAY = 1 << 16
WIDE = 16


def swap_heads(rows, n_head, me):
    if n_head != 2:
        return lax.all_to_all(rows, "head", split_axis=1, concat_axis=0, tiled=True)
    width = rows.shape[1] // 2
    kept = lax.dynamic_slice_in_dim(rows, me * width, width, 1)
    sent = lax.dynamic_slice_in_dim(rows, (1 - me) * width, width, 1)
    got = lax.ppermute(sent, "head", [(0, 1), (1, 0)])
    return jnp.where(
        me == 0, jnp.concatenate([kept, got], axis=0), jnp.concatenate([got, kept], axis=0)
    )


def swap_back(out, n_head, me):
    rows = out.shape[0] // n_head
    kept = lax.dynamic_slice_in_dim(out, me * rows, rows, 0)
    sent = lax.dynamic_slice_in_dim(out, (1 - me) * rows, rows, 0)
    return kept, lax.ppermute(sent, "head", [(0, 1), (1, 0)])


def place_columns(result, kept, got, me, at):
    width = result.shape[1] // 2
    result = lax.dynamic_update_slice(result, kept, (0, me * width + at))
    return lax.dynamic_update_slice(result, got, (0, (1 - me) * width + at))


def attend_block(q_ref, out, k_all, v_all, has_prior):
    listed = SEL * TILE
    scale = 1.0 / math.sqrt(HD)
    causal = lax.broadcasted_iota(jnp.int32, (QB, QB), 0) >= lax.broadcasted_iota(
        jnp.int32, (QB, QB), 1
    )
    for g in range(GROUP):
        q = q_ref[:, g * HD : (g + 1) * HD]
        s = lax.dot_general(
            q, k_all[...], (((1,), (1,)), ((), ())), preferred_element_type=jnp.float32
        )
        far = s[:, :listed]
        prior = jnp.where(has_prior, s[:, listed : listed + QB], NEG_FILL)
        own = jnp.where(causal, s[:, listed + QB :], NEG_FILL)
        s = jnp.concatenate([far, prior, own], axis=1)
        top = jnp.max(s, axis=1, keepdims=True)
        e = jnp.exp((s - top) * scale)
        total = jnp.sum(e, axis=1, keepdims=True)
        o = jnp.dot(e.astype(jnp.bfloat16), v_all[...], preferred_element_type=jnp.float32)
        out[:, g * HD : (g + 1) * HD] = (o / total).astype(jnp.bfloat16)


def local_rows(block, rows, prior, target):
    listed = SEL * TILE
    here = pl.ds(pl.multiple_of(block * QB, QB), QB)
    before = pl.ds(pl.multiple_of(jnp.maximum(block - 1, 0) * QB, QB), QB)

    @pl.when(block == 0)
    def _():
        target[listed : listed + QB, :] = prior[...]

    @pl.when(block > 0)
    def _():
        target[listed : listed + QB, :] = rows[before, :]

    target[listed + QB :, :] = rows[here, :]


def attend_cost(heads, rows, slots):
    keys = (SEL + 2) * TILE
    return pl.CostEstimate(
        flops=4 * heads * rows * GROUP * keys * HD,
        bytes_accessed=2 * slots * 2 * TILE * HD + 4 * heads * rows * GROUP * HD,
        transcendentals=heads * rows * GROUP * keys,
    )


def code_of(lane, place, half):
    lanes = 2 * half
    early, middle = CUTS[0], CUTS[1] - CUTS[0]
    first = lane * early + place
    near = lanes * early + lane * (PLACES - early) + place - early
    far = lanes * early + half * (PLACES - early) + (lane - half) * middle + place - early
    last = lanes * early + half * (PLACES - early + middle) + lane - half
    code = jnp.where(place < CUTS[1], far, last)
    code = jnp.where(lane < half, near, code)
    return jnp.where(place < early, first, code)


def counts_of(half):
    lanes = 2 * half
    first = lanes * CUTS[0]
    second = first + half * (PLACES - CUTS[0] + CUTS[1] - CUTS[0])
    return first, second, second + half


def plan_kernel(tiles_here, low, high, shard, ask, where, spare_where, failed, count, free):
    shards = ask.shape[0]
    heads = low.shape[0] // shards
    half = shards // 2
    me = shard[0]
    extra = counts_of(half)[2]

    def per_owner(o, carry):
        lane = o ^ me
        for p in range(WIDE):
            ask[o, p] = jnp.int32(0)
        place = jnp.int32(0)
        for h in range(heads):
            lo = low[o * heads + h]
            hi = high[o * heads + h]
            for k, (tile, has) in enumerate(((lo, lo <= hi), (hi, lo < hi))):
                ask[o, place] = h * tiles_here + tile
                code = code_of(lane, place, half)
                where[(o * heads + h) * RANKS + k] = code
                spare_where[(o * heads + h) * RANKS + k] = code
                place = place + has.astype(jnp.int32)
        ask[o, PLACES] = jnp.int32(-1)
        count[o] = place
        return carry

    lax.fori_loop(0, shards, per_owner, 0)
    other = jnp.where(me < half, half, 0)
    found = jnp.int32(0)
    for place in range(CUTS[2] - 1, CUTS[0] - 1, -1):

        def look(i, found, place=place):
            o = other + (i + me) % half
            free[found] = o * PLACES + place
            return found + (count[o] <= place).astype(jnp.int32)

        found = lax.fori_loop(0, half, look, found)

    def hand_over(i, used):
        o = other + i
        full = count[o] == PLACES

        @pl.when(full)
        def _():
            at = ((o + 1) * heads - 1) * RANKS + RANKS - 1
            spare_where[at] = extra + o
            where[at] = extra + o

            @pl.when(used < found)
            def _():
                relay = free[used] // PLACES
                place = free[used] % PLACES
                ask[o, PLACES] = relay
                ask[relay, place] = RELAY + o
                where[at] = code_of(relay ^ me, place, half)

        return used + full.astype(jnp.int32)

    used = lax.fori_loop(0, half, hand_over, jnp.int32(0))
    failed[0] = (used > found).astype(jnp.int32)


def make_plan(low, high, shard, tiles_here):
    shards, heads = low.shape
    smem = pl.BlockSpec(memory_space=pltpu.SMEM)
    half = shards // 2
    return pl.pallas_call(
        functools.partial(plan_kernel, tiles_here),
        out_shape=(
            jax.ShapeDtypeStruct((shards, WIDE), jnp.int32),
            jax.ShapeDtypeStruct((shards * heads * RANKS,), jnp.int32),
            jax.ShapeDtypeStruct((shards * heads * RANKS,), jnp.int32),
            jax.ShapeDtypeStruct((1,), jnp.int32),
        ),
        in_specs=[smem] * 3,
        out_specs=(smem,) * 4,
        scratch_shapes=[
            pltpu.SMEM((shards,), jnp.int32),
            pltpu.SMEM(((CUTS[2] - CUTS[0]) * half + 1,), jnp.int32),
        ],
        name="plan",
    )(low.reshape(-1), high.reshape(-1), shard)


def load_cache(keys, values, held, load_sem):
    loads = [
        pltpu.make_async_copy(source, held.at[kind], load_sem.at[kind])
        for kind, source in enumerate((keys, values))
    ]
    for load in loads:
        load.start()
    for load in loads:
        load.wait()


def copy_tile(held, code, tiles_here, target, sem):
    head = code // tiles_here
    tile = code % tiles_here
    rows = pl.ds(pl.multiple_of(tile * TILE, TILE), TILE)
    cols = pl.ds(pl.multiple_of(head * HD, HD), HD)
    pltpu.make_async_copy(held.at[:, rows, cols], target, sem).start()


def first_kernel(half, asked, shard, keys, values, *rest):
    outs, (held, load_sem, sem) = rest[:-3], rest[-3:]
    tiles_here = keys.shape[0] // TILE
    load_cache(keys, values, held, load_sem)
    for i, out in enumerate(outs):
        peer = (half + i) ^ shard[0]
        for p in range(out.shape[0]):
            copy_tile(held, asked[peer, p], tiles_here, out.at[p], sem)
    for out in outs:
        pltpu.make_async_copy(out, out, sem).wait()


def near_kernel(half, asked, shard, keys, values, *rest):
    outs, failed, (held, load_sem, sem, hand, filled) = rest[:-6], rest[-6], rest[-5:]
    near, given = outs[:half], outs[half:]
    tiles_here = keys.shape[0] // TILE
    me = shard[0]
    load_cache(keys, values, held, load_sem)
    for lane, out in enumerate(near):
        peer = lane ^ me
        for p in range(out.shape[0]):
            copy_tile(held, asked[peer, p], tiles_here, out.at[p], sem)
    for lane in range(half):
        filled[lane] = jnp.int32(0)
        for f in range(HAND + 1):
            hand[lane * (HAND + 1) + f] = jnp.int32(0)
    other = jnp.where(me < half, half, 0)

    def look(i, over):
        relay = asked[other + i, PLACES]
        lane = jnp.where(relay >= 0, relay ^ me, 0)
        at = jnp.minimum(filled[lane], HAND)
        hand[lane * (HAND + 1) + at] = asked[other + i, PLACES - 1]
        filled[lane] = filled[lane] + 1
        return over | ((relay >= 0) & (at == HAND)).astype(jnp.int32)

    failed[0] = lax.fori_loop(0, half, look, jnp.int32(0))
    for i, out in enumerate(given):
        for f in range(HAND):
            copy_tile(held, hand[(i + 1) * (HAND + 1) + f], tiles_here, out.at[f], sem)
    for out in outs:
        pltpu.make_async_copy(out, out, sem).wait()


def rest_kernel(half, asked, shard, keys, values, *rest):
    given, rest = rest[: half - 1], rest[half - 1 :]
    outs, (held, relayed, load_sem, sem, filled, source) = rest[:-6], rest[-6:]
    tiles_here = keys.shape[0] // TILE
    me = shard[0]
    loads = []
    for i, array in enumerate(given):
        load = pltpu.make_async_copy(array, relayed.at[i + 1], load_sem.at[2])
        load.start()
        loads.append(load)
    load_cache(keys, values, held, load_sem)
    for load in loads:
        load.wait()
    places = range(CUTS[0], CUTS[2])
    for lane in range(half):
        filled[lane] = jnp.int32(0)
    other = jnp.where(me < half, half, 0)

    def look(i, carry):
        for q, p in enumerate(places):
            code = asked[other + i, p]
            is_relay = code >= RELAY
            lane = jnp.where(is_relay, (code - RELAY) ^ me, 0)
            slot = jnp.minimum(filled[lane], HAND - 1)
            source[i * len(places) + q] = jnp.where(is_relay, RELAY + lane * HAND + slot, code)
            filled[lane] = filled[lane] + 1
        return carry

    lax.fori_loop(0, half, look, 0)
    for i in range(half):
        to = ((half + i) ^ me) - other
        for q, p in enumerate(places):
            second = p >= CUTS[1]
            out = outs[half + i].at[p - CUTS[1]] if second else outs[i].at[p - CUTS[0]]
            code = source[to * len(places) + q]

            @pl.when(code >= RELAY)
            def _():
                at = code - RELAY
                pltpu.make_async_copy(relayed.at[at // HAND, at % HAND], out, sem).start()

            @pl.when(code < RELAY)
            def _():
                copy_tile(held, code, tiles_here, out, sem)

    for out in outs:
        pltpu.make_async_copy(out, out, sem).wait()


def extra_kernel(asked, keys, values, out, held, load_sem, sem):
    tiles_here = keys.shape[0] // TILE
    load_cache(keys, values, held, load_sem)
    for i in range(out.shape[0]):
        copy_tile(held, asked[i, PLACES - 1], tiles_here, out.at[i], sem)
    pltpu.make_async_copy(out, out, sem).wait()


def gather_call(kernel, name, tables, keys, values, more, counts, flag=False, scratch=()):
    hbm = pl.BlockSpec(memory_space=pl.ANY)
    shapes = [jax.ShapeDtypeStruct((n, 2, TILE, HD), jnp.bfloat16) for n in counts]
    specs = [hbm] * len(counts)
    if flag:
        shapes.append(jax.ShapeDtypeStruct((1,), jnp.int32))
        specs.append(pl.BlockSpec(memory_space=pltpu.SMEM))
    return pl.pallas_call(
        kernel,
        out_shape=shapes,
        grid_spec=pltpu.PrefetchScalarGridSpec(
            num_scalar_prefetch=len(tables),
            grid=(),
            in_specs=[hbm] * (2 + len(more)),
            out_specs=specs,
            scratch_shapes=[pltpu.VMEM((2, *keys.shape), jnp.bfloat16), *scratch],
        ),
        compiler_params=pltpu.CompilerParams(vmem_limit_bytes=VMEM_LIMIT),
        cost_estimate=pl.CostEstimate(
            flops=0,
            bytes_accessed=4 * keys.size + 4 * sum(counts) * TILE * HD * 2,
            transcendentals=0,
        ),
        name=name,
    )(*tables, keys, values, *more)


def attend_kernel(stages, flagged, first, keep, slots, info, picks, *refs):
    q_ref, k_rows, v_rows, k_prior, v_prior = refs[:5]
    staged, k_all, v_all, sem = refs[-4:]
    arrays = refs[5 : -5 - (1 if keep else 0)]
    out = refs[-5 - (1 if keep else 0)]
    head = pl.program_id(0)
    block = pl.program_id(1)
    blocks = pl.num_programs(1)

    @pl.when((head == 0) & (block == 0))
    def _():
        copies = [
            pltpu.make_async_copy(
                arrays[i].at[pl.ds(start, count)], staged.at[pl.ds(to, count)], sem
            )
            for i, start, count, to in stages
        ]
        for copy in copies:
            copy.start()
        for copy in copies:
            copy.wait()
        if flagged is not None:
            i, to = flagged

            @pl.when(info[1] > 0)
            def _():
                copy = pltpu.make_async_copy(
                    arrays[i], staged.at[pl.ds(to, arrays[i].shape[0])], sem
                )
                copy.start()
                copy.wait()

        if keep:
            kept = refs[-5]
            for i in range(keep):
                pltpu.make_async_copy(staged.at[picks[i]], kept.at[i], sem).start()

    for j in range(SEL):
        slot = slots[((first + head) * blocks + block) * SEL + j]
        k_all[j * TILE : (j + 1) * TILE, :] = staged[slot, 0]
        v_all[j * TILE : (j + 1) * TILE, :] = staged[slot, 1]
    local_rows(block, k_rows, k_prior, k_all)
    local_rows(block, v_rows, v_prior, v_all)
    attend_block(q_ref, out, k_all, v_all, (block > 0) | (info[0] > 0))

    if keep:

        @pl.when((head == pl.num_programs(0) - 1) & (block == blocks - 1))
        def _():
            pltpu.make_async_copy(refs[-5], refs[-5], sem).wait()


def attend(slots, info, picks, q_rows, k_rows, v_rows, k_prior, v_prior, pieces, first, heads,
           flagged=None, keep=0):
    rows = q_rows.shape[0]
    blocks = rows // QB
    wide = GROUP * HD
    keys = (SEL + 2) * TILE
    arrays, stages = [], []
    for array, start, count, to in pieces:
        at = [i for i, other in enumerate(arrays) if other is array]
        if not at:
            at = [len(arrays)]
            arrays.append(array)
        stages.append((at[0], start, count, to))
    size = max(to + count for _, _, count, to in stages)
    if flagged is not None:
        array, to = flagged
        flagged = (len(arrays), to)
        arrays.append(array)
        size = max(size, to + array.shape[0])
    hbm = pl.BlockSpec(memory_space=pl.ANY)
    shapes = [jax.ShapeDtypeStruct((rows, heads * wide), jnp.bfloat16)]
    specs = [pl.BlockSpec((QB, wide), lambda h, b, *_: (b, h))]
    if keep:
        shapes.append(jax.ShapeDtypeStruct((keep, 2, TILE, HD), jnp.bfloat16))
        specs.append(hbm)
    return pl.pallas_call(
        functools.partial(attend_kernel, stages, flagged, first, keep),
        out_shape=shapes,
        grid_spec=pltpu.PrefetchScalarGridSpec(
            num_scalar_prefetch=3,
            grid=(heads, blocks),
            in_specs=[
                pl.BlockSpec((QB, wide), lambda h, b, *_: (b, first + h)),
                pl.BlockSpec((rows, HD), lambda h, b, *_: (0, first + h)),
                pl.BlockSpec((rows, HD), lambda h, b, *_: (0, first + h)),
                pl.BlockSpec((QB, HD), lambda h, b, *_: (0, first + h)),
                pl.BlockSpec((QB, HD), lambda h, b, *_: (0, first + h)),
            ]
            + [hbm] * len(arrays),
            out_specs=specs,
            scratch_shapes=[
                pltpu.VMEM((size, 2, TILE, HD), jnp.bfloat16),
                pltpu.VMEM((keys, HD), jnp.bfloat16),
                pltpu.VMEM((keys, HD), jnp.bfloat16),
                pltpu.SemaphoreType.DMA,
            ],
        ),
        compiler_params=pltpu.CompilerParams(vmem_limit_bytes=VMEM_LIMIT),
        cost_estimate=attend_cost(heads, rows, size),
        name="attend",
    )(slots, info, picks, q_rows, k_rows, v_rows, k_prior, v_prior, *arrays)


def requests(tile_lists, shards, tiles_here):
    blocks, kv_here, _ = tile_lists.shape
    listed = jnp.transpose(tile_lists, (1, 0, 2)).reshape(kv_here, blocks * SEL)
    local = listed % tiles_here
    match = (listed // tiles_here)[None] == jnp.arange(shards)[:, None, None]
    low = jnp.min(jnp.where(match, local[None], tiles_here - 1), axis=2)
    high = jnp.max(jnp.where(match, local[None], 0), axis=2)
    second = local[None] != low[:, :, None]
    return match, second, low, high


def slots_of(match, second, codes):
    picked = jnp.where(second, codes[:, :, 1:2], codes[:, :, 0:1])
    return jnp.sum(jnp.where(match, picked, 0), axis=0)


def crossed(arrays, lanes, shards):
    return [
        lax.ppermute(x, "seq", [(i, i ^ lane) for i in range(shards)])
        for x, lane in zip(arrays, lanes)
    ]


def prompt_rows(queries, new_keys, new_values, shards, n_head, me):
    q_rows = swap_heads(queries, n_head, me)
    k_rows = swap_heads(new_keys, n_head, me)
    v_rows = swap_heads(new_values, n_head, me)
    route = [(i, i + 1) for i in range(shards - 1)]
    k_prior, v_prior = lax.ppermute((k_rows[-QB:], v_rows[-QB:]), "seq", route)
    return q_rows, k_rows, v_rows, k_prior, v_prior


def packed(queries, new_keys, new_values, cache_keys, cache_values, tile_lists):
    shards = lax.axis_size("seq")
    n_head = lax.axis_size("head")
    shard = lax.axis_index("seq")
    me = lax.axis_index("head")
    blocks, kv_here, _ = tile_lists.shape
    tiles_here = cache_keys.shape[0] // TILE
    half = shards // 2
    lanes = range(half, shards)
    at = jnp.reshape(shard, (1,))

    match, second, low, high = requests(tile_lists, shards, tiles_here)
    ask, where, spare_where, failed = make_plan(low, high, at, tiles_here)
    asked = lax.all_to_all(ask, "seq", split_axis=0, concat_axis=0, tiled=True)

    dma = pltpu.SemaphoreType.DMA
    early, middle, late = CUTS[0], CUTS[1] - CUTS[0], CUTS[2] - CUTS[1]
    sent = gather_call(
        functools.partial(first_kernel, half), "gather_first", (asked, at),
        cache_keys, cache_values, (), [early] * half, scratch=(dma((3,)), dma),
    )
    got_first = crossed(sent, lanes, shards)
    asked, _ = lax.optimization_barrier((asked, sent[0]))
    *near, failed_here = gather_call(
        functools.partial(near_kernel, half), "gather_near", (asked, at),
        cache_keys, cache_values, (), [PLACES] * half + [HAND] * (half - 1), flag=True,
        scratch=(
            dma((3,)), dma, pltpu.SMEM((half * (HAND + 1),), jnp.int32),
            pltpu.SMEM((half,), jnp.int32),
        ),
    )
    near, given = near[:half], near[half:]
    given = crossed(given, range(1, half), shards)
    near = near[:1] + crossed(near[1:], range(1, half), shards)
    sent = gather_call(
        functools.partial(rest_kernel, half), "gather_rest", (asked, at),
        cache_keys, cache_values, given, [middle] * half + [late] * half,
        scratch=(
            pltpu.VMEM((half, HAND, 2, TILE, HD), jnp.bfloat16), dma((3,)), dma,
            pltpu.SMEM((half,), jnp.int32), pltpu.SMEM((half * (middle + late),), jnp.int32),
        ),
    )
    got_middle = crossed(sent[:half], lanes, shards)
    got_last = crossed(sent[half:], lanes, shards)
    flag = lax.pmax(jnp.maximum(failed, failed_here), ("seq", "head"))

    def send_extra():
        out = gather_call(
            extra_kernel, "gather_extra", (asked,), cache_keys, cache_values, (), [shards],
            scratch=(dma((3,)), dma),
        )[0]
        return lax.all_to_all(out, "seq", split_axis=0, concat_axis=0, tiled=True)

    def no_extra():
        return jnp.zeros((shards, 2, TILE, HD), jnp.bfloat16)

    extra = lax.cond(flag[0] > 0, send_extra, no_extra)

    rows = prompt_rows(queries, new_keys, new_values, shards, n_head, me)
    info = jnp.concatenate([at, flag])
    codes = where.reshape(shards, kv_here, RANKS)
    slots = slots_of(match, second, codes).reshape(-1)
    first_end, second_end, last_end = counts_of(half)
    final = jnp.where(flag[0] > 0, spare_where, where).reshape(codes.shape)
    final = final[:, kv_here - 1]
    kept = jnp.arange(shards * RANKS).reshape(shards, RANKS)
    picks = jnp.clip(final, 0, second_end - 1).reshape(-1)
    final = jnp.where(final < second_end, kept, final - second_end + shards * RANKS)
    final_slots = slots_of(match[:, -1:], second[:, -1:], final[:, None]).reshape(-1)

    pieces = [(x, 0, early, i * early) for i, x in enumerate(near)]
    pieces += [(x, 0, early, (half + i) * early) for i, x in enumerate(got_first)]
    (out_first,) = attend(slots, info, picks, *rows, pieces, 0, 2)
    later = PLACES - early
    pieces += [(x, early, later, first_end + i * later) for i, x in enumerate(near)]
    pieces += [
        (x, 0, middle, first_end + half * later + i * middle) for i, x in enumerate(got_middle)
    ]
    out_middle, held = attend(slots, info, picks, *rows, pieces, 2, 1, keep=shards * RANKS)
    pieces = [(held, 0, shards * RANKS, 0)]
    pieces += [(x, 0, late, shards * RANKS + i * late) for i, x in enumerate(got_last)]
    q_last = rows[0][:, -GROUP * HD :]
    k_last, v_last, kp_last, vp_last = (x[:, -HD:] for x in rows[1:])
    (out_last,) = attend(
        final_slots, info, picks, q_last, k_last, v_last, kp_last, vp_last, pieces, 0, 1,
        flagged=(extra, shards * RANKS + half * late),
    )

    here = out_first.shape[0] // n_head
    result = jnp.zeros((here, HQ * HD), jnp.bfloat16)
    place = 0
    for out in (out_first, out_middle, out_last):
        result = place_columns(result, *swap_back(out, n_head, me), me, place)
        place += out.shape[1]
    return result


def plain_gather_kernel(first, heads, asked, keys, values, out, held, load_sem, sem):
    shards = out.shape[0]
    loads = []
    for head in range(heads):
        cols = pl.ds((first + head) * HD, HD)
        for kind, source in enumerate((keys, values)):
            load = pltpu.make_async_copy(
                source.at[:, cols], held.at[head, kind], load_sem.at[head, kind]
            )
            load.start()
            loads.append(load)
    for head in range(heads):
        loads[2 * head].wait()
        loads[2 * head + 1].wait()

        def one(i, carry, head=head):
            peer = i // RANKS
            rank = i % RANKS
            tile = asked[peer, (first + head) * RANKS + rank]
            rows = pl.ds(pl.multiple_of(tile * TILE, TILE), TILE)
            pltpu.make_async_copy(
                held.at[head, :, rows], out.at[peer, head, rank], sem
            ).start()
            return carry

        lax.fori_loop(0, shards * RANKS, one, 0, unroll=4)
    pltpu.make_async_copy(out, out, sem).wait()


def gather_tiles(asked, keys, values, first, heads):
    shards = asked.shape[0]
    shape = (shards, heads, RANKS, 2, TILE, HD)
    return pl.pallas_call(
        functools.partial(plain_gather_kernel, first, heads),
        out_shape=jax.ShapeDtypeStruct(shape, jnp.bfloat16),
        grid_spec=pltpu.PrefetchScalarGridSpec(
            num_scalar_prefetch=1,
            grid=(),
            in_specs=[pl.BlockSpec(memory_space=pl.ANY)] * 2,
            out_specs=pl.BlockSpec(memory_space=pl.ANY),
            scratch_shapes=[
                pltpu.VMEM((heads, 2, keys.shape[0], HD), jnp.bfloat16),
                pltpu.SemaphoreType.DMA((heads, 2)),
                pltpu.SemaphoreType.DMA,
            ],
        ),
        compiler_params=pltpu.CompilerParams(vmem_limit_bytes=VMEM_LIMIT),
        cost_estimate=pl.CostEstimate(
            flops=0, bytes_accessed=4 * math.prod(shape), transcendentals=0
        ),
        name="gather_tiles",
    )(asked, keys, values)


def plain(queries, new_keys, new_values, cache_keys, cache_values, tile_lists):
    shards = lax.axis_size("seq")
    n_head = lax.axis_size("head")
    shard = lax.axis_index("seq")
    me = lax.axis_index("head")
    blocks, kv_here, _ = tile_lists.shape
    tiles_here = cache_keys.shape[0] // TILE

    match, second, low, high = requests(tile_lists, shards, tiles_here)
    wanted = jnp.stack([low, high], axis=2).reshape(shards, kv_here * RANKS)
    asked = lax.all_to_all(wanted, "seq", split_axis=0, concat_axis=0, tiled=True)
    codes = jnp.arange(shards * RANKS).reshape(shards, 1, RANKS)
    slots = slots_of(match, second, jnp.broadcast_to(codes, (shards, kv_here, RANKS))).reshape(-1)
    rows = prompt_rows(queries, new_keys, new_values, shards, n_head, me)
    info = jnp.concatenate([jnp.reshape(shard, (1,)), jnp.zeros((1,), jnp.int32)])
    picks = jnp.zeros((1,), jnp.int32)
    outs = []
    for head in range(kv_here):
        sent = gather_tiles(asked, cache_keys, cache_values, head, 1)
        got = lax.all_to_all(sent, "seq", split_axis=0, concat_axis=0, tiled=True)
        got = got.reshape(shards * RANKS, 2, TILE, HD)
        outs += attend(
            slots, info, picks, *rows, [(got, 0, shards * RANKS, 0)], head, 1
        )
    whole = jnp.concatenate(outs, axis=1)
    return lax.all_to_all(whole, "head", split_axis=0, concat_axis=1, tiled=True)


def on_device(queries, new_keys, new_values, cache_keys, cache_values, tile_lists):
    shards = lax.axis_size("seq")
    fits = tile_lists.shape[1] * RANKS == PLACES and shards >= 4 and shards & (shards - 1) == 0
    plan = packed if fits and lax.axis_size("head") == 2 else plain
    return plan(queries, new_keys, new_values, cache_keys, cache_values, tile_lists)


def solution(mesh):
    return jax.shard_map(
        on_device,
        mesh=mesh,
        in_specs=(
            P(("seq", "head"), None),
            P(("seq", "head"), None),
            P(("seq", "head"), None),
            P("seq", "head"),
            P("seq", "head"),
            P("seq", "head", None),
        ),
        out_specs=P(("seq", "head"), None),
        check_vma=False,
    )
```

time: 240 us -> 346 us (1.44)
  the two profiles are of different devices: /device:TPU:10 before, /device:TPU:0 now
where the time goes in v3:
time: 346 us; the launch traced here: 344 us
  waiting for transfers between devices  80.7 us (23%)
  starting transfers between devices  79 us (23%)
  blocking collectives  71 us (21%)
  Pallas kernels  62.3 us (18%)
  local copies, waits for them, and re-layouts  38.3 us (11%)
  other arithmetic  10.4 us (3%)
    ppermute x38, waiting for transfers between devices, crossed(): lax.ppermute(x, 'seq', [(i, i ^ lane) for i in range(shards)])  73.7 us
    ppermute x38, starting transfers between devices, crossed(): lax.ppermute(x, 'seq', [(i, i ^ lane) for i in range(shards)])  63.6 us
    pmax x1, blocking collectives, packed(): flag = lax.pmax(jnp.maximum(failed, failed_here), ('seq', 'head'))  57.3 us
    pallas_call x3, Pallas kernels, attend(): pl.pallas_call(functools.partial(attend_kernel, stages, flagged, first, k...  44.6 us
    unnamed x132, local copies, waits for them, and re-layouts  15.9 us
    pallas_call x3, Pallas kernels, gather_call(): pl.pallas_call(kernel, out_shape=shapes, grid_spec=pltpu.PrefetchScalarGr...  14.9 us
    all_to_all x1, blocking collectives, packed(): asked = lax.all_to_all(ask, 'seq', split_axis=0, concat_axis=0, tiled=True)  13.7 us
  transfers between devices with their start and end apart: 46, of which 10 were waited for; matrix products, arithmetic and copies ran while one was open for 8% of the time, Pallas kernels for 15%

profile of v3, /device:TPU:0, one launch (start us, length us, event | category | flops | bytes accessed | tf_op | source)
XLA Modules:
  0.0 344.4 jit_solution(6646332156074411423)
XLA Ops:
  2.6 2.9 plan.1
  5.4 13.7 %all_to_all.16 = s32[16,1,16]{2,1,0:T(1,128)S(1)} all-to-all(s32[16,1,16]{2,1,0:T(1,128)} %bitcast.14), channel_id=1, replica_groups=mesh['seq'=16,'head'=2] {'seq'}, dimensions={0} | all-to-all | bytes 2048 | tf_op jit(solution)/shard_map/all_to_all | solution.py:500
  19.1 4.6 %gather_first.1 = (bf16[4,2,128,128]{3,2,1,0:T(8,128)(2,1)S(1)}, bf16[4,2,128,128]{3,2,1,0:T(8,128)(2,1)S(1)}, bf16[4,2,128,128]{3,2,1,0:T(8,128)(2,1)S(1)}, bf1...) custom-call(s32[16,16]{1,0:T(8,128)S(1)} %bitcast.9, ...), custom_call_target="tpu_custom_call" | custom-call | bytes 8388608 | tf_op jit(solution)/shard_map/gather_first/pallas_call | solution.py:330
  23.8 3.5 %gather_near.1 = (bf16[8,2,128,128]{3,2,1,0:T(8,128)(2,1)S(1)}, bf16[8,2,128,128]{3,2,1,0:T(8,128)(2,1)}, bf16[8,2,128,128]{3,2,1,0:T(8,128)(2,1)}, bf16[8,2,128...) custom-call(s32[16,16]{1,0:T(8,128)S(1)} %bitcast.10, ...), custom_call_target="tpu_custom_call" | custom-call | bytes 15335424 | tf_op jit(solution)/shard_map/gather_near/pallas_call | solution.py:330
  32.2 1.4 collective-permute-start.23
  34.0 1.1 collective-permute-start.25
  35.7 1.8 constant_dynamic-slice_fusion.6
  37.5 1.8 constant_dynamic-slice_fusion.4
  39.6 1.5 collective-permute-start.1
  41.1 1.9 collective-permute-done.23.rest_2_
  43.0 1.5 collective-permute-start.2
  45.1 2.0 collective-permute-start.13
  47.0 3.3 collective-permute-done.26.rest_5_
  51.0 1.5 constant_dynamic-slice_fusion.8
  52.5 10.3 %collective-permute-done.27.rest_6_ = bf16[3,2,128,128]{3,2,1,0:T(8,128)(2,1)S(1)} collective-permute-done((bf16[3,2,128,128]{3,2,1,0:T(8,128)(2,1)S(1)}, bf16[3,2,128,128]{3,2,1,0:T(8,128)(2,1)S(1)}, u32[]{:S(2)}, u32[]{:S(2)}) %collective-permute-start.27) | collective-permute-done | bytes 196640 | tf_op jit(solution)/shard_map/ppermute | solution.py:473
  63.5 1.5 collective-permute-start
  65.0 2.7 collective-permute-start.14
  67.7 2.4 collective-permute-start.16
  70.3 1.8 collective-permute-start.17
  72.5 26.8 %collective-permute-done.14.refs_15_ = bf16[4,2,128,128]{3,2,1,0:T(8,128)(2,1)S(1)} collective-permute-done((bf16[4,2,128,128]{3,2,1,0:T(8,128)(2,1)S(1)}, bf16[4,2,128,128]{3,2,1,0:T(8,128)(2,1)S(1)}, u32[]{:S(2)}, u32[]{:S(2)}) %collective-permute-start.14) | collective-permute-done | bytes 262176 | tf_op jit(solution)/shard_map/ppermute | solution.py:473
  99.3 4.6 %collective-permute-done.15.refs_16_ = bf16[4,2,128,128]{3,2,1,0:T(8,128)(2,1)S(1)} collective-permute-done((bf16[4,2,128,128]{3,2,1,0:T(8,128)(2,1)S(1)}, bf16[4,2,128,128]{3,2,1,0:T(8,128)(2,1)S(1)}, u32[]{:S(2)}, u32[]{:S(2)}) %collective-permute-start.15) | collective-permute-done | bytes 262176 | tf_op jit(solution)/shard_map/ppermute | solution.py:473
  103.9 1.6 collective-permute-start.6
  106.1 3.9 %collective-permute-start.19 = (bf16[4,2,128,128]{3,2,1,0:T(8,128)(2,1)}, bf16[4,2,128,128]{3,2,1,0:T(8,128)(2,1)}, u32[]{:S(2)}, u32[]{:S(2)}) collective-permute-start(bf16[4,2,128,128]{3,2,1,0:T(8,128)(2,1)} %get-tuple-element.85), channel_id=1, source_target_pairs={{0,30},{2,28},{4,26},{6,24},{8,22},{10,20},{12,18},{14,16},{16,14}... | collective-permute-start | bytes 786440 | tf_op jit(solution)/shard_map/ppermute | solution.py:473
  111.5 57.3 %pmax.7 = s32[1]{0:T(128)} all-reduce(s32[1]{0:T(128)S(6)} %max.11), channel_id=1, replica_groups=mesh['seq'=16,'head'=2] {'seq','head'}, use_global_device_ids=true, to_apply=%region_3.4 | all-reduce | flops 1 | bytes 8 | tf_op jit(solution)/shard_map/pmax | solution.py:531
  169.6 1.2 maximum_select_fusion.1.refs_1_
  171.5 1.4 maximum_select_fusion.2.refs_2_
  173.6 1.3 collective-permute-start.3
  174.9 5.6 %collective-permute-start.4 = (bf16[128,512]{1,0:T(8,128)(2,1)}, bf16[128,512]{1,0:T(8,128)(2,1)}, u32[]{:S(2)}, u32[]{:S(2)}) collective-permute-start(bf16[128,512]{1,0:T(8,128)(2,1)} %slice.60), channel_id=1, source_target_pairs={{0,2},{2,4},{4,6},{6,8},{8,10},{10,12},{12,14},{14,16},{16,18},{18... | collective-permute-start | bytes 393224 | tf_op jit(solution)/shard_map/ppermute | solution.py:483
  182.3 2.9 collective-permute-start.8
  185.2 1.2 collective-permute-start.10
  186.4 1.4 collective-permute-start.11
  187.8 2.0 compare_select_fusion
  191.4 0.9 copy-done.4
  192.3 0.9 copy-done.6
  193.2 0.9 copy-done.8
  195.1 0.9 copy-done.12
  196.0 0.9 copy-done.14
  197.9 6.7 %gather_rest.1 = (bf16[2,2,128,128]{3,2,1,0:T(8,128)(2,1)S(1)}, bf16[2,2,128,128]{3,2,1,0:T(8,128)(2,1)S(1)}, bf16[2,2,128,128]{3,2,1,0:T(8,128)(2,1)S(1)}, bf16...) custom-call(s32[16,16]{1,0:T(8,128)} %bitcast.11, ...), custom_call_target="tpu_custom_call" | custom-call | bytes 7340032 | tf_op jit(solution)/shard_map/gather_rest/pallas_call | solution.py:330
  204.7 3.9 %maximum_select_fusion.refs_0_ = bf16[512,2048]{1,0:T(8,128)(2,1)} fusion(bf16[256,2048]{1,0:T(8,128)(2,1)} %collective-permute-done, bf16[256,2048]{1,0:T(8,128)(2,1)S(1)} %copy-done.50, pred[]{:T(512)S(6)} %eq.23), kind=kLoop, calls=%fused_computation | loop fusion | flops 9437184 | bytes 4194305 | tf_op jit(solution)/shard_map/jit(_where)/select_n | solution.py:36
  208.6 2.6 collective-permute-start.28
  211.4 2.1 collective-permute-start.30
  213.4 16.6 %collective-permute-done.10.refs_11_ = bf16[8,2,128,128]{3,2,1,0:T(8,128)(2,1)} collective-permute-done((bf16[8,2,128,128]{3,2,1,0:T(8,128)(2,1)}, bf16[8,2,128,128]{3,2,1,0:T(8,128)(2,1)}, u32[]{:S(2)}, u32[]{:S(2)}) %collective-permute-start.10) | collective-permute-done | bytes 524320 | tf_op jit(solution)/shard_map/ppermute | solution.py:473
  230.1 9.8 %collective-permute-done.11.refs_12_ = bf16[8,2,128,128]{3,2,1,0:T(8,128)(2,1)} collective-permute-done((bf16[8,2,128,128]{3,2,1,0:T(8,128)(2,1)}, bf16[8,2,128,128]{3,2,1,0:T(8,128)(2,1)}, u32[]{:S(2)}, u32[]{:S(2)}) %collective-permute-start.11) | collective-permute-done | bytes 524320 | tf_op jit(solution)/shard_map/ppermute | solution.py:473
  239.9 21.6 %attend.3 = bf16[512,1024]{1,0:T(8,128)(2,1)} custom-call(s32[192]{0:T(256)S(1)} %reshape.113.slots, s32[2]{0:T(128)S(1)} %pad_add_fusion.info, s32[32]{0:T(128)S(1)} %min.12.picks, bf16[512,2048]{1,0:T(8,128)(2,1)} %maximum_select_fusion.refs_0_, bf16[512,512]{1,0:T(8,128)(2,1)S(1)} %maximum_select_fusion.1.refs_1_, ...), custom_call_target="tpu_custom_call" | custom-call | flops 3758096384 | bytes 6291456 | tf_op jit(solution)/shard_map/attend/pallas_call | solution.py:427
  261.7 0.9 copy-done.53
  263.6 2.0 collective-permute-start.20
  266.2 2.1 collective-permute-start.32
  269.0 1.2 collective-permute-start.33
  270.9 2.4 collective-permute-start.34
  273.9 2.3 collective-permute-start.35
  276.3 1.2 conditional.1
  276.3 1.2 broadcast.81
  278.3 6.1 %collective-permute-start.37 = (bf16[1,2,128,128]{3,2,1,0:T(8,128)(2,1)S(1)}, bf16[1,2,128,128]{3,2,1,0:T(8,128)(2,1)S(1)}, u32[]{:S(2)}, u32[]{:S(2)}) collective-permute-start(bf16[1,2,128,128]{3,2,1,0:T(8,128)(2,1)S(1)} %copy-done.47), channel_id=1, source_target_pairs={{0,16},{2,18},{4,20},{6,22},{8,24},{10,26},{12,28},{14,30},{16,0},... | collective-permute-start | bytes 196616 | tf_op jit(solution)/shard_map/ppermute | solution.py:473
  284.5 0.9 collective-permute-start.38
  285.4 4.0 %collective-permute-start.39 = (bf16[1,2,128,128]{3,2,1,0:T(8,128)(2,1)S(1)}, bf16[1,2,128,128]{3,2,1,0:T(8,128)(2,1)S(1)}, u32[]{:S(2)}, u32[]{:S(2)}) collective-permute-start(bf16[1,2,128,128]{3,2,1,0:T(8,128)(2,1)S(1)} %copy-done.43), channel_id=1, source_target_pairs={{0,20},{2,22},{4,16},{6,18},{8,28},{10,30},{12,24},{14,26},{16,4},... | collective-permute-start | bytes 196616 | tf_op jit(solution)/shard_map/ppermute | solution.py:473
  289.4 4.6 %collective-permute-start.40 = (bf16[1,2,128,128]{3,2,1,0:T(8,128)(2,1)S(1)}, bf16[1,2,128,128]{3,2,1,0:T(8,128)(2,1)S(1)}, u32[]{:S(2)}, u32[]{:S(2)}) collective-permute-start(bf16[1,2,128,128]{3,2,1,0:T(8,128)(2,1)S(1)} %copy-done.41), channel_id=1, source_target_pairs={{0,22},{2,20},{4,18},{6,16},{8,30},{10,28},{12,26},{14,24},{16,6},... | collective-permute-start | bytes 196616 | tf_op jit(solution)/shard_map/ppermute | solution.py:473
  294.1 12.8 %attend.4 = (bf16[512,512]{1,0:T(8,128)(2,1)S(1)}, bf16[32,2,128,128]{3,2,1,0:T(8,128)(2,1)}) custom-call(s32[192]{0:T(256)S(1)} %reshape.113.slots, s32[2]{0:T(128)S(1)} %pad_add_fusion.info, s32[32]{0:T(128)S(1)} %min.12.picks, bf16[512,2048]{1,0:T(8,128)(2,1)} %maximum_select_fusion.refs_0_, bf16[512,512]{1,0:T(8,128)(2,1)} %copy-done, ...), custom_call_target="tpu_custom_call" | custom-call | flops 1879048192 | bytes 8388608 | tf_op jit(solution)/shard_map/attend/pallas_call | solution.py:427
  307.0 5.3 %collective-permute-start.41 = (bf16[1,2,128,128]{3,2,1,0:T(8,128)(2,1)S(1)}, bf16[1,2,128,128]{3,2,1,0:T(8,128)(2,1)S(1)}, u32[]{:S(2)}, u32[]{:S(2)}) collective-permute-start(bf16[1,2,128,128]{3,2,1,0:T(8,128)(2,1)S(1)} %copy-done.39), channel_id=1, source_target_pairs={{0,24},{2,26},{4,28},{6,30},{8,16},{10,18},{12,20},{14,22},{16,8},... | collective-permute-start | bytes 196616 | tf_op jit(solution)/shard_map/ppermute | solution.py:473
  312.3 1.9 constant_dynamic-update-slice_fusion.2
  315.9 3.3 collective-permute-start.44
  322.0 1.1 slice.65.refs_0_
  323.1 10.2 %attend.5 = bf16[512,512]{1,0:T(8,128)(2,1)S(1)} custom-call(s32[48]{0:T(128)S(1)} %select_reduce_fusion.3.slots, s32[2]{0:T(128)S(1)} %pad_add_fusion.info, s32[32]{0:T(128)S(1)} %min.12.picks, bf16[512,512]{1,0:T(8,128)(2,1)S(1)} %slice.65.refs_0_, bf16[512,128]{1,0:T(8,128)(2,1)S(1)} %slice.66.refs_1_, bf16[512,128]{1,0:T(8,128)(2,1)S(1)} %slice.67.refs_2_, ...), custom_call_target="tpu_custom_call" | custom-call | flops 1879048192 | bytes 4718592 | tf_op jit(solution)/shard_map/attend/pallas_call | solution.py:427
  334.8 2.0 collective-permute-start.45
  336.8 6.9 %collective-permute-done.45 = bf16[256,512]{1,0:T(8,128)(2,1)S(1)} collective-permute-done((bf16[256,512]{1,0:T(8,128)(2,1)S(1)}, bf16[256,512]{1,0:T(8,128)(2,1)S(1)}, u32[]{:S(2)}, u32[]{:S(2)}) %collective-permute-start.45) | collective-permute-done | bytes 262176 | tf_op jit(solution)/shard_map/ppermute | solution.py:45
  (213 shorter events, 30.2 us)
Async XLA Ops:
  0.8 109.2 %copy-start.61 = (s32[4,48]{1,0:T(4,128)}, s32[4,48]{1,0:T(4,128)S(1)}, u32[]{:S(2)}) copy-start(s32[4,48]{1,0:T(4,128)S(1)} %get-tuple-element.132) | copy-start | bytes 2308
  1.0 109.0 %copy-start.63 = (s32[16,4]{0,1:T(4,128)}, s32[16,4]{0,1:T(4,128)S(1)}, u32[]{:S(2)}) copy-start(s32[16,4]{0,1:T(4,128)S(1)} %get-tuple-element.114) | copy-start | bytes 772
  31.7 208.2 %copy-start.2 = (bf16[8,2,128,128]{3,2,1,0:T(8,128)(2,1)}, bf16[8,2,128,128]{3,2,1,0:T(8,128)(2,1)S(1)}, u32[]{:S(2)}) copy-start(bf16[8,2,128,128]{3,2,1,0:T(8,128)(2,1)S(1)} %get-tuple-element.71.refs_5_) | copy-start | bytes 1572868
  31.7 3.5 %collective-permute-start.21 = (bf16[3,2,128,128]{3,2,1,0:T(8,128)(2,1)}, bf16[3,2,128,128]{3,2,1,0:T(8,128)(2,1)S(1)}, u32[]{:S(2)}, u32[]{:S(2)}) collective-permute-start(bf16[3,2,128,128]{3,2,1,0:T(8,128)(2,1)} %get-tuple-element.86), channel_id=1, source_target_pairs={{0,2},{2,0},{4,6},{6,4},{8,10},{10,8},{12,14},{14,12},{16,18},{18,... | collective-permute-start | bytes 589832 | tf_op jit(solution)/shard_map/ppermute | solution.py:473
  31.7 19.3 %copy-start.51 = (bf16[256,4096]{1,0:T(8,128)(2,1)S(1)}, bf16[256,4096]{1,0:T(8,128)(2,1)}, u32[]{:S(2)}) copy-start(bf16[256,4096]{1,0:T(8,128)(2,1)} %param.8) | copy-start | bytes 6291460
  31.7 7.9 %collective-permute-start.22 = (bf16[3,2,128,128]{3,2,1,0:T(8,128)(2,1)}, bf16[3,2,128,128]{3,2,1,0:T(8,128)(2,1)S(1)}, u32[]{:S(2)}, u32[]{:S(2)}) collective-permute-start(bf16[3,2,128,128]{3,2,1,0:T(8,128)(2,1)} %copy-done.31), channel_id=1, source_target_pairs={{0,4},{2,6},{4,0},{6,2},{8,12},{10,14},{12,8},{14,10},{16,20},{18,... | collective-permute-start | bytes 589832 | tf_op jit(solution)/shard_map/ppermute | solution.py:473
  32.2 10.8 %collective-permute-start.23 = (bf16[3,2,128,128]{3,2,1,0:T(8,128)(2,1)}, bf16[3,2,128,128]{3,2,1,0:T(8,128)(2,1)S(1)}, u32[]{:S(2)}, u32[]{:S(2)}) collective-permute-start(bf16[3,2,128,128]{3,2,1,0:T(8,128)(2,1)} %copy-done.30), channel_id=1, source_target_pairs={{0,6},{2,4},{4,2},{6,0},{8,14},{10,12},{12,10},{14,8},{16,22},{18,... | collective-permute-start | bytes 589832 | tf_op jit(solution)/shard_map/ppermute | solution.py:473
  33.5 11.0 %collective-permute-start.24 = (bf16[3,2,128,128]{3,2,1,0:T(8,128)(2,1)}, bf16[3,2,128,128]{3,2,1,0:T(8,128)(2,1)S(1)}, u32[]{:S(2)}, u32[]{:S(2)}) collective-permute-start(bf16[3,2,128,128]{3,2,1,0:T(8,128)(2,1)} %copy-done.29), channel_id=1, source_target_pairs={{0,8},{2,10},{4,12},{6,14},{8,0},{10,2},{12,4},{14,6},{16,24},{18,... | collective-permute-start | bytes 589832 | tf_op jit(solution)/shard_map/ppermute | solution.py:473
  34.0 11.0 %collective-permute-start.25 = (bf16[3,2,128,128]{3,2,1,0:T(8,128)(2,1)}, bf16[3,2,128,128]{3,2,1,0:T(8,128)(2,1)S(1)}, u32[]{:S(2)}, u32[]{:S(2)}) collective-permute-start(bf16[3,2,128,128]{3,2,1,0:T(8,128)(2,1)} %copy-done.28), channel_id=1, source_target_pairs={{0,10},{2,8},{4,14},{6,12},{8,2},{10,0},{12,6},{14,4},{16,26},{18,... | collective-permute-start | bytes 589832 | tf_op jit(solution)/shard_map/ppermute | solution.py:473
  35.2 17.3 %copy-start.3 = (bf16[3,2,128,128]{3,2,1,0:T(8,128)(2,1)}, bf16[3,2,128,128]{3,2,1,0:T(8,128)(2,1)S(1)}, u32[]{:S(2)}) copy-start(bf16[3,2,128,128]{3,2,1,0:T(8,128)(2,1)S(1)} %collective-permute-done.21.rest_0_) | copy-start | bytes 589828
  35.2 15.1 %collective-permute-start.26 = (bf16[3,2,128,128]{3,2,1,0:T(8,128)(2,1)S(1)}, bf16[3,2,128,128]{3,2,1,0:T(8,128)(2,1)S(1)}, u32[]{:S(2)}, u32[]{:S(2)}) collective-permute-start(bf16[3,2,128,128]{3,2,1,0:T(8,128)(2,1)S(1)} %get-tuple-element.91), channel_id=1, source_target_pairs={{0,12},{2,14},{4,8},{6,10},{8,4},{10,6},{12,0},{14,2},{16,28},{18,... | collective-permute-start | bytes 589832 | tf_op jit(solution)/shard_map/ppermute | solution.py:473
  39.6 25.4 %collective-permute-start.1 = (bf16[256,512]{1,0:T(8,128)(2,1)S(1)}, bf16[256,512]{1,0:T(8,128)(2,1)S(1)}, u32[]{:S(2)}, u32[]{:S(2)}) collective-permute-start(bf16[256,512]{1,0:T(8,128)(2,1)S(1)} %get-tuple-element.126), channel_id=1, source_target_pairs={{0,1},{1,0},{2,3},{3,2},{4,5},{5,4},{6,7},{7,6},{8,9},{9,8},{10,11... | collective-permute-start | bytes 786440 | tf_op jit(solution)/shard_map/ppermute | solution.py:35
  43.0 24.7 %collective-permute-start.2 = (bf16[256,512]{1,0:T(8,128)(2,1)S(1)}, bf16[256,512]{1,0:T(8,128)(2,1)S(1)}, u32[]{:S(2)}, u32[]{:S(2)}) collective-permute-start(bf16[256,512]{1,0:T(8,128)(2,1)S(1)} %get-tuple-element.124), channel_id=1, source_target_pairs={{0,1},{1,0},{2,3},{3,2},{4,5},{5,4},{6,7},{7,6},{8,9},{9,8},{10,11... | collective-permute-start | bytes 786440 | tf_op jit(solution)/shard_map/ppermute | solution.py:35
  44.6 23.2 %collective-permute-start.12 = (bf16[4,2,128,128]{3,2,1,0:T(8,128)(2,1)S(1)}, bf16[4,2,128,128]{3,2,1,0:T(8,128)(2,1)S(1)}, u32[]{:S(2)}, u32[]{:S(2)}) collective-permute-start(bf16[4,2,128,128]{3,2,1,0:T(8,128)(2,1)S(1)} %get-tuple-element.67), channel_id=1, source_target_pairs={{0,16},{2,18},{4,20},{6,22},{8,24},{10,26},{12,28},{14,30},{16,0},... | collective-permute-start | bytes 786440 | tf_op jit(solution)/shard_map/ppermute | solution.py:473
  45.1 25.2 %collective-permute-start.13 = (bf16[4,2,128,128]{3,2,1,0:T(8,128)(2,1)S(1)}, bf16[4,2,128,128]{3,2,1,0:T(8,128)(2,1)S(1)}, u32[]{:S(2)}, u32[]{:S(2)}) collective-permute-start(bf16[4,2,128,128]{3,2,1,0:T(8,128)(2,1)S(1)} %get-tuple-element.79), channel_id=1, source_target_pairs={{0,18},{2,16},{4,22},{6,20},{8,26},{10,24},{12,30},{14,28},{16,2},... | collective-permute-start | bytes 786440 | tf_op jit(solution)/shard_map/ppermute | solution.py:473
  51.0 21.1 %copy-start.65 = (s32[128]{0:T(128)S(1)}, s32[128]{0:T(128)}, u32[]{:S(2)}) copy-start(s32[128]{0:T(128)} %get-tuple-element.64) | copy-start | bytes 1540
  51.0 118.6 %copy-start.55 = (bf16[256,512]{1,0:T(8,128)(2,1)S(1)}, bf16[256,512]{1,0:T(8,128)(2,1)}, u32[]{:S(2)}) copy-start(bf16[256,512]{1,0:T(8,128)(2,1)} %get-tuple-element.125) | copy-start | bytes 786436
  51.0 11.8 %collective-permute-start.27 = (bf16[3,2,128,128]{3,2,1,0:T(8,128)(2,1)S(1)}, bf16[3,2,128,128]{3,2,1,0:T(8,128)(2,1)S(1)}, u32[]{:S(2)}, u32[]{:S(2)}) collective-permute-start(bf16[3,2,128,128]{3,2,1,0:T(8,128)(2,1)S(1)} %get-tuple-element.92), channel_id=1, source_target_pairs={{0,14},{2,12},{4,10},{6,8},{8,6},{10,4},{12,2},{14,0},{16,30},{18,... | collective-permute-start | bytes 589832 | tf_op jit(solution)/shard_map/ppermute | solution.py:473
  63.5 122.9 %collective-permute-start = (bf16[256,2048]{1,0:T(8,128)(2,1)}, bf16[256,2048]{1,0:T(8,128)(2,1)}, u32[]{:S(2)}, u32[]{:S(2)}) collective-permute-start(bf16[256,2048]{1,0:T(8,128)(2,1)} %get-tuple-element.116), channel_id=1, source_target_pairs={{0,1},{1,0},{2,3},{3,2},{4,5},{5,4},{6,7},{7,6},{8,9},{9,8},{10,11... | collective-permute-start | bytes 3145736 | tf_op jit(solution)/shard_map/ppermute | solution.py:35
  65.0 34.3 %collective-permute-start.14 = (bf16[4,2,128,128]{3,2,1,0:T(8,128)(2,1)S(1)}, bf16[4,2,128,128]{3,2,1,0:T(8,128)(2,1)S(1)}, u32[]{:S(2)}, u32[]{:S(2)}) collective-permute-start(bf16[4,2,128,128]{3,2,1,0:T(8,128)(2,1)S(1)} %get-tuple-element.80), channel_id=1, source_target_pairs={{0,20},{2,22},{4,16},{6,18},{8,28},{10,30},{12,24},{14,26},{16,4},... | collective-permute-start | bytes 786440 | tf_op jit(solution)/shard_map/ppermute | solution.py:473
  67.7 36.1 %collective-permute-start.15 = (bf16[4,2,128,128]{3,2,1,0:T(8,128)(2,1)S(1)}, bf16[4,2,128,128]{3,2,1,0:T(8,128)(2,1)S(1)}, u32[]{:S(2)}, u32[]{:S(2)}) collective-permute-start(bf16[4,2,128,128]{3,2,1,0:T(8,128)(2,1)S(1)} %get-tuple-element.81), channel_id=1, source_target_pairs={{0,22},{2,20},{4,18},{6,16},{8,30},{10,28},{12,26},{14,24},{16,6},... | collective-permute-start | bytes 786440 | tf_op jit(solution)/shard_map/ppermute | solution.py:473
  67.7 37.7 %collective-permute-start.16 = (bf16[4,2,128,128]{3,2,1,0:T(8,128)(2,1)S(1)}, bf16[4,2,128,128]{3,2,1,0:T(8,128)(2,1)S(1)}, u32[]{:S(2)}, u32[]{:S(2)}) collective-permute-start(bf16[4,2,128,128]{3,2,1,0:T(8,128)(2,1)S(1)} %get-tuple-element.82), channel_id=1, source_target_pairs={{0,24},{2,26},{4,28},{6,30},{8,16},{10,18},{12,20},{14,22},{16,8},... | collective-permute-start | bytes 786440 | tf_op jit(solution)/shard_map/ppermute | solution.py:473
  70.3 35.9 %collective-permute-start.17 = (bf16[4,2,128,128]{3,2,1,0:T(8,128)(2,1)S(1)}, bf16[4,2,128,128]{3,2,1,0:T(8,128)(2,1)S(1)}, u32[]{:S(2)}, u32[]{:S(2)}) collective-permute-start(bf16[4,2,128,128]{3,2,1,0:T(8,128)(2,1)S(1)} %get-tuple-element.83), channel_id=1, source_target_pairs={{0,26},{2,24},{4,30},{6,28},{8,18},{10,16},{12,22},{14,20},{16,10}... | collective-permute-start | bytes 786440 | tf_op jit(solution)/shard_map/ppermute | solution.py:473
  99.3 85.9 %collective-permute-start.5 = (bf16[8,2,128,128]{3,2,1,0:T(8,128)(2,1)}, bf16[8,2,128,128]{3,2,1,0:T(8,128)(2,1)}, u32[]{:S(2)}, u32[]{:S(2)}) collective-permute-start(bf16[8,2,128,128]{3,2,1,0:T(8,128)(2,1)} %get-tuple-element.72), channel_id=1, source_target_pairs={{0,2},{2,0},{4,6},{6,4},{8,10},{10,8},{12,14},{14,12},{16,18},{18,... | collective-permute-start | bytes 1572872 | tf_op jit(solution)/shard_map/ppermute | solution.py:473
  103.9 81.3 %collective-permute-start.6 = (bf16[8,2,128,128]{3,2,1,0:T(8,128)(2,1)}, bf16[8,2,128,128]{3,2,1,0:T(8,128)(2,1)}, u32[]{:S(2)}, u32[]{:S(2)}) collective-permute-start(bf16[8,2,128,128]{3,2,1,0:T(8,128)(2,1)} %get-tuple-element.73), channel_id=1, source_target_pairs={{0,4},{2,6},{4,0},{6,2},{8,12},{10,14},{12,8},{14,10},{16,20},{18,... | collective-permute-start | bytes 1572872 | tf_op jit(solution)/shard_map/ppermute | solution.py:473
  105.4 68.2 %collective-permute-start.18 = (bf16[4,2,128,128]{3,2,1,0:T(8,128)(2,1)}, bf16[4,2,128,128]{3,2,1,0:T(8,128)(2,1)S(1)}, u32[]{:S(2)}, u32[]{:S(2)}) collective-permute-start(bf16[4,2,128,128]{3,2,1,0:T(8,128)(2,1)} %get-tuple-element.84), channel_id=1, source_target_pairs={{0,28},{2,30},{4,24},{6,26},{8,20},{10,22},{12,16},{14,18},{16,12}... | collective-permute-start | bytes 786440 | tf_op jit(solution)/shard_map/ppermute | solution.py:473
  106.1 68.8 %collective-permute-start.19 = (bf16[4,2,128,128]{3,2,1,0:T(8,128)(2,1)}, bf16[4,2,128,128]{3,2,1,0:T(8,128)(2,1)}, u32[]{:S(2)}, u32[]{:S(2)}) collective-permute-start(bf16[4,2,128,128]{3,2,1,0:T(8,128)(2,1)} %get-tuple-element.85), channel_id=1, source_target_pairs={{0,30},{2,28},{4,26},{6,24},{8,22},{10,20},{12,18},{14,16},{16,14}... | collective-permute-start | bytes 786440 | tf_op jit(solution)/shard_map/ppermute | solution.py:473
  170.8 69.1 %copy-start = (bf16[512,512]{1,0:T(8,128)(2,1)}, bf16[512,512]{1,0:T(8,128)(2,1)S(1)}, u32[]{:S(2)}) copy-start(bf16[512,512]{1,0:T(8,128)(2,1)S(1)} %maximum_select_fusion.1.refs_1_) | copy-start | bytes 1572868
  172.9 67.0 %copy-start.1 = (bf16[512,512]{1,0:T(8,128)(2,1)}, bf16[512,512]{1,0:T(8,128)(2,1)S(1)}, u32[]{:S(2)}) copy-start(bf16[512,512]{1,0:T(8,128)(2,1)S(1)} %maximum_select_fusion.2.refs_2_) | copy-start | bytes 1572868
  173.6 8.3 %collective-permute-start.3 = (bf16[128,512]{1,0:T(8,128)(2,1)}, bf16[128,512]{1,0:T(8,128)(2,1)S(1)}, u32[]{:S(2)}, u32[]{:S(2)}) collective-permute-start(bf16[128,512]{1,0:T(8,128)(2,1)} %slice.59), channel_id=1, source_target_pairs={{0,2},{2,4},{4,6},{6,8},{8,10},{10,12},{12,14},{14,16},{16,18},{18... | collective-permute-start | bytes 393224 | tf_op jit(solution)/shard_map/ppermute | solution.py:483
  174.9 7.3 %collective-permute-start.4 = (bf16[128,512]{1,0:T(8,128)(2,1)}, bf16[128,512]{1,0:T(8,128)(2,1)}, u32[]{:S(2)}, u32[]{:S(2)}) collective-permute-start(bf16[128,512]{1,0:T(8,128)(2,1)} %slice.60), channel_id=1, source_target_pairs={{0,2},{2,4},{4,6},{6,8},{8,10},{10,12},{12,14},{14,16},{16,18},{18... | collective-permute-start | bytes 393224 | tf_op jit(solution)/shard_map/ppermute | solution.py:483
  182.0 26.7 %collective-permute-start.7 = (bf16[8,2,128,128]{3,2,1,0:T(8,128)(2,1)}, bf16[8,2,128,128]{3,2,1,0:T(8,128)(2,1)}, u32[]{:S(2)}, u32[]{:S(2)}) collective-permute-start(bf16[8,2,128,128]{3,2,1,0:T(8,128)(2,1)} %copy-done.27), channel_id=1, source_target_pairs={{0,6},{2,4},{4,2},{6,0},{8,14},{10,12},{12,10},{14,8},{16,22},{18,... | collective-permute-start | bytes 1572872 | tf_op jit(solution)/shard_map/ppermute | solution.py:473
  182.3 28.9 %collective-permute-start.8 = (bf16[8,2,128,128]{3,2,1,0:T(8,128)(2,1)}, bf16[8,2,128,128]{3,2,1,0:T(8,128)(2,1)}, u32[]{:S(2)}, u32[]{:S(2)}) collective-permute-start(bf16[8,2,128,128]{3,2,1,0:T(8,128)(2,1)} %copy-done.26), channel_id=1, source_target_pairs={{0,8},{2,10},{4,12},{6,14},{8,0},{10,2},{12,4},{14,6},{16,24},{18,... | collective-permute-start | bytes 1572872 | tf_op jit(solution)/shard_map/ppermute | solution.py:473
  185.2 26.2 %collective-permute-start.9 = (bf16[8,2,128,128]{3,2,1,0:T(8,128)(2,1)}, bf16[8,2,128,128]{3,2,1,0:T(8,128)(2,1)}, u32[]{:S(2)}, u32[]{:S(2)}) collective-permute-start(bf16[8,2,128,128]{3,2,1,0:T(8,128)(2,1)} %get-tuple-element.76), channel_id=1, source_target_pairs={{0,10},{2,8},{4,14},{6,12},{8,2},{10,0},{12,6},{14,4},{16,26},{18,... | collective-permute-start | bytes 1572872 | tf_op jit(solution)/shard_map/ppermute | solution.py:473
  185.2 44.8 %collective-permute-start.10 = (bf16[8,2,128,128]{3,2,1,0:T(8,128)(2,1)}, bf16[8,2,128,128]{3,2,1,0:T(8,128)(2,1)}, u32[]{:S(2)}, u32[]{:S(2)}) collective-permute-start(bf16[8,2,128,128]{3,2,1,0:T(8,128)(2,1)} %get-tuple-element.77), channel_id=1, source_target_pairs={{0,12},{2,14},{4,8},{6,10},{8,4},{10,6},{12,0},{14,2},{16,28},{18,... | collective-permute-start | bytes 1572872 | tf_op jit(solution)/shard_map/ppermute | solution.py:473
  186.4 53.5 %collective-permute-start.11 = (bf16[8,2,128,128]{3,2,1,0:T(8,128)(2,1)}, bf16[8,2,128,128]{3,2,1,0:T(8,128)(2,1)}, u32[]{:S(2)}, u32[]{:S(2)}) collective-permute-start(bf16[8,2,128,128]{3,2,1,0:T(8,128)(2,1)} %get-tuple-element.78), channel_id=1, source_target_pairs={{0,14},{2,12},{4,10},{6,8},{8,6},{10,4},{12,2},{14,0},{16,30},{18,... | collective-permute-start | bytes 1572872 | tf_op jit(solution)/shard_map/ppermute | solution.py:473
  208.6 56.9 %collective-permute-start.28 = (bf16[2,2,128,128]{3,2,1,0:T(8,128)(2,1)S(1)}, bf16[2,2,128,128]{3,2,1,0:T(8,128)(2,1)S(1)}, u32[]{:S(2)}, u32[]{:S(2)}) collective-permute-start(bf16[2,2,128,128]{3,2,1,0:T(8,128)(2,1)S(1)} %get-tuple-element.93), channel_id=1, source_target_pairs={{0,16},{2,18},{4,20},{6,22},{8,24},{10,26},{12,28},{14,30},{16,0},... | collective-permute-start | bytes 393224 | tf_op jit(solution)/shard_map/ppermute | solution.py:473
  211.2 57.1 %collective-permute-start.29 = (bf16[2,2,128,128]{3,2,1,0:T(8,128)(2,1)S(1)}, bf16[2,2,128,128]{3,2,1,0:T(8,128)(2,1)S(1)}, u32[]{:S(2)}, u32[]{:S(2)}) collective-permute-start(bf16[2,2,128,128]{3,2,1,0:T(8,128)(2,1)S(1)} %get-tuple-element.94), channel_id=1, source_target_pairs={{0,18},{2,16},{4,22},{6,20},{8,26},{10,24},{12,30},{14,28},{16,2},... | collective-permute-start | bytes 393224 | tf_op jit(solution)/shard_map/ppermute | solution.py:473
  211.4 58.8 %collective-permute-start.30 = (bf16[2,2,128,128]{3,2,1,0:T(8,128)(2,1)S(1)}, bf16[2,2,128,128]{3,2,1,0:T(8,128)(2,1)S(1)}, u32[]{:S(2)}, u32[]{:S(2)}) collective-permute-start(bf16[2,2,128,128]{3,2,1,0:T(8,128)(2,1)S(1)} %get-tuple-element.95), channel_id=1, source_target_pairs={{0,20},{2,22},{4,16},{6,18},{8,28},{10,30},{12,24},{14,26},{16,4},... | collective-permute-start | bytes 393224 | tf_op jit(solution)/shard_map/ppermute | solution.py:473
  230.1 43.2 %collective-permute-start.31 = (bf16[2,2,128,128]{3,2,1,0:T(8,128)(2,1)S(1)}, bf16[2,2,128,128]{3,2,1,0:T(8,128)(2,1)S(1)}, u32[]{:S(2)}, u32[]{:S(2)}) collective-permute-start(bf16[2,2,128,128]{3,2,1,0:T(8,128)(2,1)S(1)} %get-tuple-element.96), channel_id=1, source_target_pairs={{0,22},{2,20},{4,18},{6,16},{8,30},{10,28},{12,26},{14,24},{16,6},... | collective-permute-start | bytes 393224 | tf_op jit(solution)/shard_map/ppermute | solution.py:473
  263.6 43.4 %collective-permute-start.20 = (bf16[256,1024]{1,0:T(8,128)(2,1)}, bf16[256,1024]{1,0:T(8,128)(2,1)}, u32[]{:S(2)}, u32[]{:S(2)}) collective-permute-start(bf16[256,1024]{1,0:T(8,128)(2,1)} %get-tuple-element.117), channel_id=1, source_target_pairs={{0,1},{1,0},{2,3},{3,2},{4,5},{5,4},{6,7},{7,6},{8,9},{9,8},{10,11... | collective-permute-start | bytes 1572872 | tf_op jit(solution)/shard_map/ppermute | solution.py:45
  266.2 12.1 %collective-permute-start.32 = (bf16[2,2,128,128]{3,2,1,0:T(8,128)(2,1)}, bf16[2,2,128,128]{3,2,1,0:T(8,128)(2,1)S(1)}, u32[]{:S(2)}, u32[]{:S(2)}) collective-permute-start(bf16[2,2,128,128]{3,2,1,0:T(8,128)(2,1)} %get-tuple-element.97), channel_id=1, source_target_pairs={{0,24},{2,26},{4,28},{6,30},{8,16},{10,18},{12,20},{14,22},{16,8},... | collective-permute-start | bytes 393224 | tf_op jit(solution)/shard_map/ppermute | solution.py:473
  269.0 15.5 %collective-permute-start.33 = (bf16[2,2,128,128]{3,2,1,0:T(8,128)(2,1)}, bf16[2,2,128,128]{3,2,1,0:T(8,128)(2,1)S(1)}, u32[]{:S(2)}, u32[]{:S(2)}) collective-permute-start(bf16[2,2,128,128]{3,2,1,0:T(8,128)(2,1)} %get-tuple-element.98), channel_id=1, source_target_pairs={{0,26},{2,24},{4,30},{6,28},{8,18},{10,16},{12,22},{14,20},{16,10}... | collective-permute-start | bytes 393224 | tf_op jit(solution)/shard_map/ppermute | solution.py:473
  270.9 14.6 %collective-permute-start.34 = (bf16[2,2,128,128]{3,2,1,0:T(8,128)(2,1)}, bf16[2,2,128,128]{3,2,1,0:T(8,128)(2,1)S(1)}, u32[]{:S(2)}, u32[]{:S(2)}) collective-permute-start(bf16[2,2,128,128]{3,2,1,0:T(8,128)(2,1)} %get-tuple-element.99), channel_id=1, source_target_pairs={{0,28},{2,30},{4,24},{6,26},{8,20},{10,22},{12,16},{14,18},{16,12}... | collective-permute-start | bytes 393224 | tf_op jit(solution)/shard_map/ppermute | solution.py:473
  273.9 15.5 %collective-permute-start.35 = (bf16[2,2,128,128]{3,2,1,0:T(8,128)(2,1)}, bf16[2,2,128,128]{3,2,1,0:T(8,128)(2,1)S(1)}, u32[]{:S(2)}, u32[]{:S(2)}) collective-permute-start(bf16[2,2,128,128]{3,2,1,0:T(8,128)(2,1)} %get-tuple-element.100), channel_id=1, source_target_pairs={{0,30},{2,28},{4,26},{6,24},{8,22},{10,20},{12,18},{14,16},{16,14}... | collective-permute-start | bytes 393224 | tf_op jit(solution)/shard_map/ppermute | solution.py:473
  276.3 17.8 %copy-start.18 = (bf16[2,2,128,128]{3,2,1,0:T(8,128)(2,1)S(1)}, bf16[2,2,128,128]{3,2,1,0:T(8,128)(2,1)}, u32[]{:S(2)}) copy-start(bf16[2,2,128,128]{3,2,1,0:T(8,128)(2,1)} %copy-done.17) | copy-start | bytes 393220
  276.3 17.8 %copy-start.20 = (bf16[2,2,128,128]{3,2,1,0:T(8,128)(2,1)S(1)}, bf16[2,2,128,128]{3,2,1,0:T(8,128)(2,1)}, u32[]{:S(2)}) copy-start(bf16[2,2,128,128]{3,2,1,0:T(8,128)(2,1)} %copy-done.19) | copy-start | bytes 393220
  276.3 17.8 %copy-start.22 = (bf16[2,2,128,128]{3,2,1,0:T(8,128)(2,1)S(1)}, bf16[2,2,128,128]{3,2,1,0:T(8,128)(2,1)}, u32[]{:S(2)}) copy-start(bf16[2,2,128,128]{3,2,1,0:T(8,128)(2,1)} %copy-done.21) | copy-start | bytes 393220
  276.3 17.7 %copy-start.24 = (bf16[2,2,128,128]{3,2,1,0:T(8,128)(2,1)S(1)}, bf16[2,2,128,128]{3,2,1,0:T(8,128)(2,1)}, u32[]{:S(2)}) copy-start(bf16[2,2,128,128]{3,2,1,0:T(8,128)(2,1)} %copy-done.23) | copy-start | bytes 393220
  278.3 36.6 %collective-permute-start.37 = (bf16[1,2,128,128]{3,2,1,0:T(8,128)(2,1)S(1)}, bf16[1,2,128,128]{3,2,1,0:T(8,128)(2,1)S(1)}, u32[]{:S(2)}, u32[]{:S(2)}) collective-permute-start(bf16[1,2,128,128]{3,2,1,0:T(8,128)(2,1)S(1)} %copy-done.47), channel_id=1, source_target_pairs={{0,16},{2,18},{4,20},{6,22},{8,24},{10,26},{12,28},{14,30},{16,0},... | collective-permute-start | bytes 196616 | tf_op jit(solution)/shard_map/ppermute | solution.py:473
  284.5 30.6 %collective-permute-start.38 = (bf16[1,2,128,128]{3,2,1,0:T(8,128)(2,1)S(1)}, bf16[1,2,128,128]{3,2,1,0:T(8,128)(2,1)S(1)}, u32[]{:S(2)}, u32[]{:S(2)}) collective-permute-start(bf16[1,2,128,128]{3,2,1,0:T(8,128)(2,1)S(1)} %copy-done.45), channel_id=1, source_target_pairs={{0,18},{2,16},{4,22},{6,20},{8,26},{10,24},{12,30},{14,28},{16,2},... | collective-permute-start | bytes 196616 | tf_op jit(solution)/shard_map/ppermute | solution.py:473
  285.4 30.5 %collective-permute-start.39 = (bf16[1,2,128,128]{3,2,1,0:T(8,128)(2,1)S(1)}, bf16[1,2,128,128]{3,2,1,0:T(8,128)(2,1)S(1)}, u32[]{:S(2)}, u32[]{:S(2)}) collective-permute-start(bf16[1,2,128,128]{3,2,1,0:T(8,128)(2,1)S(1)} %copy-done.43), channel_id=1, source_target_pairs={{0,20},{2,22},{4,16},{6,18},{8,28},{10,30},{12,24},{14,26},{16,4},... | collective-permute-start | bytes 196616 | tf_op jit(solution)/shard_map/ppermute | solution.py:473
  289.4 17.5 %copy-start.39 = (bf16[1,2,128,128]{3,2,1,0:T(8,128)(2,1)S(1)}, bf16[1,2,128,128]{3,2,1,0:T(8,128)(2,1)}, u32[]{:S(2)}) copy-start(bf16[1,2,128,128]{3,2,1,0:T(8,128)(2,1)} %copy-done.38) | copy-start | bytes 196612
  289.4 29.8 %collective-permute-start.40 = (bf16[1,2,128,128]{3,2,1,0:T(8,128)(2,1)S(1)}, bf16[1,2,128,128]{3,2,1,0:T(8,128)(2,1)S(1)}, u32[]{:S(2)}, u32[]{:S(2)}) collective-permute-start(bf16[1,2,128,128]{3,2,1,0:T(8,128)(2,1)S(1)} %copy-done.41), channel_id=1, source_target_pairs={{0,22},{2,20},{4,18},{6,16},{8,30},{10,28},{12,26},{14,24},{16,6},... | collective-permute-start | bytes 196616 | tf_op jit(solution)/shard_map/ppermute | solution.py:473
  294.1 20.8 %copy-start.37 = (bf16[1,2,128,128]{3,2,1,0:T(8,128)(2,1)S(1)}, bf16[1,2,128,128]{3,2,1,0:T(8,128)(2,1)}, u32[]{:S(2)}) copy-start(bf16[1,2,128,128]{3,2,1,0:T(8,128)(2,1)} %copy-done.36) | copy-start | bytes 196612
  294.1 21.1 %copy-start.35 = (bf16[1,2,128,128]{3,2,1,0:T(8,128)(2,1)S(1)}, bf16[1,2,128,128]{3,2,1,0:T(8,128)(2,1)}, u32[]{:S(2)}) copy-start(bf16[1,2,128,128]{3,2,1,0:T(8,128)(2,1)} %copy-done.34) | copy-start | bytes 196612
  294.1 21.8 %copy-start.33 = (bf16[1,2,128,128]{3,2,1,0:T(8,128)(2,1)S(1)}, bf16[1,2,128,128]{3,2,1,0:T(8,128)(2,1)}, u32[]{:S(2)}) copy-start(bf16[1,2,128,128]{3,2,1,0:T(8,128)(2,1)} %copy-done.32) | copy-start | bytes 196612
  306.9 16.2 %copy-start.25 = (bf16[32,2,128,128]{3,2,1,0:T(8,128)(2,1)S(1)}, bf16[32,2,128,128]{3,2,1,0:T(8,128)(2,1)}, u32[]{:S(2)}) copy-start(bf16[32,2,128,128]{3,2,1,0:T(8,128)(2,1)} %get-tuple-element.102.refs_5_) | copy-start | bytes 6291460
  307.0 16.1 %collective-permute-start.41 = (bf16[1,2,128,128]{3,2,1,0:T(8,128)(2,1)S(1)}, bf16[1,2,128,128]{3,2,1,0:T(8,128)(2,1)S(1)}, u32[]{:S(2)}, u32[]{:S(2)}) collective-permute-start(bf16[1,2,128,128]{3,2,1,0:T(8,128)(2,1)S(1)} %copy-done.39), channel_id=1, source_target_pairs={{0,24},{2,26},{4,28},{6,30},{8,16},{10,18},{12,20},{14,22},{16,8},... | collective-permute-start | bytes 196616 | tf_op jit(solution)/shard_map/ppermute | solution.py:473
  314.9 8.1 %collective-permute-start.42 = (bf16[1,2,128,128]{3,2,1,0:T(8,128)(2,1)S(1)}, bf16[1,2,128,128]{3,2,1,0:T(8,128)(2,1)S(1)}, u32[]{:S(2)}, u32[]{:S(2)}) collective-permute-start(bf16[1,2,128,128]{3,2,1,0:T(8,128)(2,1)S(1)} %copy-done.37), channel_id=1, source_target_pairs={{0,26},{2,24},{4,30},{6,28},{8,18},{10,16},{12,22},{14,20},{16,10}... | collective-permute-start | bytes 196616 | tf_op jit(solution)/shard_map/ppermute | solution.py:473
  315.1 7.9 %collective-permute-start.43 = (bf16[1,2,128,128]{3,2,1,0:T(8,128)(2,1)S(1)}, bf16[1,2,128,128]{3,2,1,0:T(8,128)(2,1)S(1)}, u32[]{:S(2)}, u32[]{:S(2)}) collective-permute-start(bf16[1,2,128,128]{3,2,1,0:T(8,128)(2,1)S(1)} %copy-done.35), channel_id=1, source_target_pairs={{0,28},{2,30},{4,24},{6,26},{8,20},{10,22},{12,16},{14,18},{16,12}... | collective-permute-start | bytes 196616 | tf_op jit(solution)/shard_map/ppermute | solution.py:473
  315.9 7.1 %collective-permute-start.44 = (bf16[1,2,128,128]{3,2,1,0:T(8,128)(2,1)S(1)}, bf16[1,2,128,128]{3,2,1,0:T(8,128)(2,1)S(1)}, u32[]{:S(2)}, u32[]{:S(2)}) collective-permute-start(bf16[1,2,128,128]{3,2,1,0:T(8,128)(2,1)S(1)} %copy-done.33), channel_id=1, source_target_pairs={{0,30},{2,28},{4,26},{6,24},{8,22},{10,20},{12,18},{14,16},{16,14}... | collective-permute-start | bytes 196616 | tf_op jit(solution)/shard_map/ppermute | solution.py:473
  319.3 14.1 %collective-permute-start.36 = (bf16[256,512]{1,0:T(8,128)(2,1)S(1)}, bf16[256,512]{1,0:T(8,128)(2,1)S(1)}, u32[]{:S(2)}, u32[]{:S(2)}) collective-permute-start(bf16[256,512]{1,0:T(8,128)(2,1)S(1)} %get-tuple-element.121), channel_id=1, source_target_pairs={{0,1},{1,0},{2,3},{3,2},{4,5},{5,4},{6,7},{7,6},{8,9},{9,8},{10,11... | collective-permute-start | bytes 786440 | tf_op jit(solution)/shard_map/ppermute | solution.py:45
  334.8 8.9 %collective-permute-start.45 = (bf16[256,512]{1,0:T(8,128)(2,1)S(1)}, bf16[256,512]{1,0:T(8,128)(2,1)S(1)}, u32[]{:S(2)}, u32[]{:S(2)}) collective-permute-start(bf16[256,512]{1,0:T(8,128)(2,1)S(1)} %get-tuple-element.119), channel_id=1, source_target_pairs={{0,1},{1,0},{2,3},{3,2},{4,5},{5,4},{6,7},{7,6},{8,9},{9,8},{10,11... | collective-permute-start | bytes 786440 | tf_op jit(solution)/shard_map/ppermute | solution.py:45
  (48 other events, 221.5 us)
